TPU v7x, 32 devices: a whole 2x2x4 slice. The times are simulated.
32 devices in a mesh: shot: 2 (over y), gy: 4 (over z), gx: 4 (over x, core).
Axes of the slice: x: 2, y: 2, z: 4, core: 2. Of those that a mesh axis runs over, the one named last changes fastest.
Arguments:
- pressure_now: float32 [128, 64, 512], P(('shot', 'gx'), 'gy'), parts along dimension 0, may hold values from -6 to 6
- pressure_old: float32 [128, 64, 512], P(('shot', 'gx'), 'gy'), parts along dimension 0, may hold values from -6 to 6
- classes: int32 [128, 64, 512], P(('shot', 'gx'), 'gy'), parts along dimension 0, may hold values from 0 to 15
- class_table: float32 [16], replicated, may hold values from 0.02 to 0.19
- wavelet: float32 [512], P('shot'), parts along dimension 0, may hold values from -12 to 12
- source_cells: int32 [8], P('shot'), parts along dimension 0, may hold values from 0 to 2097151
- samples: int32 [8], P('shot'), parts along dimension 0, may hold values from 0 to 255
Outputs:
- pressure_next: float32 [128, 64, 512], P(('shot', 'gx'), 'gy'), parts along dimension 0
- pressure_mid: float32 [128, 64, 512], P(('shot', 'gx'), 'gy'), parts along dimension 0
- snapshot_code: float32 [128, 64, 512], P(('shot', 'gx'), 'gy'), parts along dimension 0
There are 2 independent parts, one for each index of `shot`. A program takes and returns all parts, laid end to end along the dimension named above; an argument that names none is the same for every part. Nothing has to cross between parts.
Inputs may be any that keep to these rules, and one draw needn't show every extreme that they name: `source_cells`: decoded as ix * 64 * 512 + iy * 512 + iz.
All inputs are finite; a program needn't handle non-finite values.
Results may differ from a plain program's by a relative error of at most 0.0003.
Values sent between devices are 32-bit elements; how exact they have to be, the bound alone decides.
A program may use at most 64 MiB of HBM per device.

v0:
```python
import jax
import jax.numpy as jnp
from jax import lax
from jax.sharding import PartitionSpec as P

STENCIL_WEIGHTS = (-205.0 / 72.0, 8.0 / 5.0, -1.0 / 5.0, 8.0 / 315.0, -1.0 / 560.0)
LIFT_ALPHA = -1.586134342
LIFT_BETA = -0.05298011854
LIFT_GAMMA = 0.8829110762
LIFT_DELTA = 0.4435068522
LIFT_SCALE = 1.149604398
DEAD_ZONE = 0.25
QUANT_STEP = 0.5


def padded_2(block, sides, width):
    for axis, dim in sides:
        count = lax.axis_size(axis)
        forward = [(i, i + 1) for i in range(count - 1)]
        backward = [(target, source) for source, target in forward]
        low = lax.ppermute(
            lax.slice_in_dim(block, block.shape[dim] - width, None, axis=dim), axis, forward
        )
        high = lax.ppermute(lax.slice_in_dim(block, 0, width, axis=dim), axis, backward)
        block = jnp.concatenate([low, block, high], axis=dim)
    return block


def laplace(extended):
    size_x = extended.shape[0] - 8
    size_y = extended.shape[1] - 8
    depth = extended.shape[2]
    depth_padded = jnp.pad(extended[:, 4 : 4 + size_y, :], ((0, 0), (0, 0), (4, 4)))
    center = extended[4 : 4 + size_x, 4 : 4 + size_y, :]
    summed = 3.0 * STENCIL_WEIGHTS[0] * center
    for offset in range(1, 5):
        beside = (
            extended[4 + offset : 4 + offset + size_x, 4 : 4 + size_y, :]
            + extended[4 - offset : 4 - offset + size_x, 4 : 4 + size_y, :]
        )
        beside = (
            beside
            + extended[4 : 4 + size_x, 4 + offset : 4 + offset + size_y, :]
            + extended[4 : 4 + size_x, 4 - offset : 4 - offset + size_y, :]
        )
        beside = (
            beside
            + depth_padded[4 : 4 + size_x, :, 4 + offset : 4 + offset + depth]
            + depth_padded[4 : 4 + size_x, :, 4 - offset : 4 - offset + depth]
        )
        summed = summed + STENCIL_WEIGHTS[offset] * beside
    return summed


def cut_range(field, start, limit, along):
    return lax.slice_in_dim(field, start, limit, 1, along)


def lift_core(padded, along):
    length = padded.shape[along]
    even = lax.slice_in_dim(padded, 0, length, 2, along)
    odd = lax.slice_in_dim(padded, 1, length, 2, along)
    half = even.shape[along]
    odd_one = cut_range(odd, 0, half - 1, along) + LIFT_ALPHA * (
        cut_range(even, 0, half - 1, along) + cut_range(even, 1, half, along)
    )
    even_one = cut_range(even, 1, half - 1, along) + LIFT_BETA * (
        cut_range(odd_one, 0, half - 2, along) + cut_range(odd_one, 1, half - 1, along)
    )
    odd_two = cut_range(odd_one, 1, half - 2, along) + LIFT_GAMMA * (
        cut_range(even_one, 0, half - 3, along) + cut_range(even_one, 1, half - 2, along)
    )
    even_two = cut_range(even_one, 1, half - 3, along) + LIFT_DELTA * (
        cut_range(odd_two, 0, half - 4, along) + cut_range(odd_two, 1, half - 3, along)
    )
    low_band = even_two / LIFT_SCALE
    high_band = cut_range(odd_two, 1, half - 3, along) * LIFT_SCALE
    joined = jnp.stack([low_band, high_band], along + 1)
    shape = low_band.shape[:along] + (2 * low_band.shape[along],) + low_band.shape[along + 1 :]
    return joined.reshape(shape)


def reflect_lift(field, along):
    widths = [(0, 0)] * field.ndim
    widths[along] = (4, 4)
    return lift_core(jnp.pad(field, widths, mode="reflect"), along)


def mend_edges(field, extended, along, at_first, at_last):
    length = field.shape[along]
    left_pad = jnp.where(
        at_first, jnp.flip(cut_range(field, 1, 5, along), along), cut_range(extended, 0, 4, along)
    )
    right_pad = jnp.where(
        at_last,
        jnp.flip(cut_range(field, length - 5, length - 1, along), along),
        cut_range(extended, length + 4, length + 8, along),
    )
    return jnp.concatenate([left_pad, field, right_pad], along)


def quantize(values):
    return jnp.sign(values) * jnp.maximum(jnp.abs(values) - DEAD_ZONE, 0.0) / QUANT_STEP


def lookup(classes, class_table):
    courant = jnp.zeros(classes.shape, jnp.float32)
    for material in range(class_table.shape[0]):
        courant = jnp.where(classes == material, class_table[material], courant)
    return courant


def source_block(places, amplitude, start_x, start_y, size_x, size_y, depth):
    cell_x, cell_y, cell_z = places
    match_x = ((jnp.arange(size_x, dtype=jnp.int32) + start_x)[:, None] == cell_x[None, :]).astype(
        jnp.float32
    )
    match_y = ((jnp.arange(size_y, dtype=jnp.int32) + start_y)[:, None] == cell_y[None, :]).astype(
        jnp.float32
    )
    match_z = (jnp.arange(depth, dtype=jnp.int32)[:, None] == cell_z[None, :]).astype(jnp.float32)
    return jnp.einsum(
        "as,bs,cs->abc",
        match_x,
        match_y * amplitude[None, :],
        match_z,
        precision=lax.Precision.HIGHEST,
    )


def shards(pressure_now, pressure_old, classes, class_table, wavelet, source_cells, samples):
    rows_x, rows_y, depth = pressure_now.shape
    all_y = rows_y * lax.axis_size("gy")
    wave_len = wavelet.shape[0]
    places = (source_cells // (all_y * depth), source_cells // depth % all_y, source_cells % depth)
    start_x = lax.axis_index("gx") * rows_x
    start_y = lax.axis_index("gy") * rows_y
    first_x = lax.axis_index("gx") == 0
    last_x = lax.axis_index("gx") == lax.axis_size("gx") - 1
    first_y = lax.axis_index("gy") == 0
    last_y = lax.axis_index("gy") == lax.axis_size("gy") - 1
    courant = lookup(classes, class_table)
    amp_first = wavelet[(samples + 0) % wave_len]
    amp_second = wavelet[(samples + 1) % wave_len]

    def advance(field, older, amplitude):
        extended = padded_2(field, (("gy", 1), ("gx", 0)), 4)
        source = source_block(places, amplitude, start_x, start_y, rows_x, rows_y, depth)
        return 2.0 * field - older + courant * laplace(extended) + source

    pressure_mid = advance(pressure_now, pressure_old, amp_first)
    pressure_next = advance(pressure_mid, pressure_now, amp_second)
    lifted = reflect_lift(pressure_next, 2)
    rim_x = padded_2(lifted, (("gx", 0),), 4)
    lifted = lift_core(mend_edges(lifted, rim_x, 0, first_x, last_x), 0)
    rim_y = padded_2(lifted, (("gy", 1),), 4)
    lifted = lift_core(mend_edges(lifted, rim_y, 1, first_y, last_y), 1)
    snapshot_code = quantize(lifted)
    return (pressure_next, pressure_mid, snapshot_code)


def solution(mesh):
    placed = (
        P(("shot", "gx"), "gy", None),
        P(("shot", "gx"), "gy", None),
        P(("shot", "gx"), "gy", None),
        P(),
        P("shot"),
        P("shot"),
        P("shot"),
    )
    return jax.shard_map(
        shards,
        mesh=mesh,
        in_specs=placed,
        out_specs=(
            P(("shot", "gx"), "gy", None),
            P(("shot", "gx"), "gy", None),
            P(("shot", "gx"), "gy", None),
        ),
        check_vma=False,
    )
```

profile of v0, /device:TPU:1, one launch (start us, length us, event | category | flops | bytes accessed | tf_op | source)
XLA Modules:
  0.0 137.9 jit_solution(17068739779333369813)
XLA Ops:
  0.7 1.1 fusion.122
  1.9 4.0 %collective-permute-start = (f32[16,4,512]{2,0,1:T(8,128)S(1)}, f32[16,4,512]{2,0,1:T(8,128)S(1)}, u32[]{:S(2)}, u32[]{:S(2)}) collective-permute-start(f32[16,4,512]{2,0,1:T(8,128)S(1)} %copy.205), channel_id=1, source_target_pairs={{0,4},{4,8},{8,12},{1,5},{5,9},{9,13},{2,6},{6,10},{10,14},{3,7},{... | collective-permute-start | bytes 393224 | tf_op jit(solution)/shard_map/ppermute | solution.py:21
  6.0 1.3 collective-permute-start.1
  7.3 0.7 compare_select_fusion.2
  8.0 0.7 and_select_fusion.1
  8.6 0.6 gather_fusion.1
  9.3 0.6 gather_fusion
  10.0 0.7 fusion.123
  10.8 0.3 constant_dynamic-update-slice_fusion.4
  11.1 0.6 collective-permute-done.1
  11.8 4.1 %collective-permute-start.2 = (f32[4,24,512]{2,0,1:T(4,128)S(1)}, f32[4,24,512]{2,0,1:T(4,128)S(1)}, u32[]{:S(2)}, u32[]{:S(2)}) collective-permute-start(f32[4,24,512]{2,0,1:T(4,128)S(1)} %get-tuple-element.24), channel_id=1, source_target_pairs={{1,0},{2,1},{3,2},{5,4},{6,5},{7,6},{9,8},{10,9},{11,10},{13,12},{... | collective-permute-start | bytes 589832 | tf_op jit(solution)/shard_map/ppermute | solution.py:24
  16.0 3.0 %collective-permute-start.3 = (f32[4,24,512]{2,0,1:T(4,128)S(1)}, f32[4,24,512]{2,0,1:T(4,128)S(1)}, u32[]{:S(2)}, u32[]{:S(2)}) collective-permute-start(f32[4,24,512]{2,0,1:T(4,128)S(1)} %get-tuple-element.25), channel_id=1, source_target_pairs={{0,1},{1,2},{2,3},{4,5},{5,6},{6,7},{8,9},{9,10},{10,11},{12,13},{... | collective-permute-start | bytes 589832 | tf_op jit(solution)/shard_map/ppermute | solution.py:21
  19.1 1.3 collective-permute-done.2
  20.4 1.2 collective-permute-done.3
  21.6 0.5 select_maximum_fusion.4
  22.1 12.9 %fusion.1 = f32[16,16,512]{2,0,1:T(8,128)S(1)} fusion(f32[16,24,512]{2,0,1:T(8,128)S(1)} %get-tuple-element.50, f32[4,24,512]{2,0,1:T(4,128)S(1)} %collective-permute-done.3, f32[4,24,512]{2,0,1:T(4,128)S(1)} %collective-permute-done.2, f32[24,16,520]{2,0,1:T(8,128)S(1)} %select_maximum_fusion.4, f32[16,20,512]{2,0,1:T(8,128)S(1)} %get-tuple-element.42, ...), kind=kOutput, calls=%fused_computation.19 | convolution fusion | flops 15993856 | bytes 11666000 | tf_op jit(solution)/shard_map/as,bs,cs->abc/dot_general | solution.py:122
  35.1 1.3 collective-permute-start.5
  36.4 4.0 %collective-permute-start.4 = (f32[16,4,512]{2,0,1:T(8,128)S(1)}, f32[16,4,512]{2,0,1:T(8,128)S(1)}, u32[]{:S(2)}, u32[]{:S(2)}) collective-permute-start(f32[16,4,512]{2,0,1:T(8,128)S(1)} %get-tuple-element.39), channel_id=1, source_target_pairs={{0,4},{4,8},{8,12},{1,5},{5,9},{9,13},{2,6},{6,10},{10,14},{3,7},{... | collective-permute-start | bytes 393224 | tf_op jit(solution)/shard_map/ppermute | solution.py:21
  40.4 0.4 collective-permute-done.5
  40.8 1.5 %collective-permute-done.4 = f32[16,4,512]{2,0,1:T(8,128)S(1)} collective-permute-done((f32[16,4,512]{2,0,1:T(8,128)S(1)}, f32[16,4,512]{2,0,1:T(8,128)S(1)}, u32[]{:S(2)}, u32[]{:S(2)}) %collective-permute-start.4) | collective-permute-done | bytes 131104 | tf_op jit(solution)/shard_map/ppermute | solution.py:21
  42.4 5.5 %collective-permute-start.7 = (f32[4,24,512]{2,0,1:T(4,128)S(1)}, f32[4,24,512]{2,0,1:T(4,128)S(1)}, u32[]{:S(2)}, u32[]{:S(2)}) collective-permute-start(f32[4,24,512]{2,0,1:T(4,128)S(1)} %get-tuple-element.22), channel_id=1, source_target_pairs={{0,1},{1,2},{2,3},{4,5},{5,6},{6,7},{8,9},{9,10},{10,11},{12,13},{... | collective-permute-start | bytes 589832 | tf_op jit(solution)/shard_map/ppermute | solution.py:21
  47.9 2.1 %collective-permute-start.6 = (f32[4,24,512]{2,0,1:T(4,128)S(1)}, f32[4,24,512]{2,0,1:T(4,128)S(1)}, u32[]{:S(2)}, u32[]{:S(2)}) collective-permute-start(f32[4,24,512]{2,0,1:T(4,128)S(1)} %get-tuple-element.23), channel_id=1, source_target_pairs={{1,0},{2,1},{3,2},{5,4},{6,5},{7,6},{9,8},{10,9},{11,10},{13,12},{... | collective-permute-start | bytes 589832 | tf_op jit(solution)/shard_map/ppermute | solution.py:24
  50.0 0.5 collective-permute-done.7
  50.5 4.4 %collective-permute-done.6 = f32[4,24,512]{2,0,1:T(4,128)S(1)} collective-permute-done((f32[4,24,512]{2,0,1:T(4,128)S(1)}, f32[4,24,512]{2,0,1:T(4,128)S(1)}, u32[]{:S(2)}, u32[]{:S(2)}) %collective-permute-start.6) | collective-permute-done | bytes 196640 | tf_op jit(solution)/shard_map/ppermute | solution.py:24
  54.9 0.5 select_maximum_fusion
  55.4 0.2 pad_maximum_fusion
  55.6 12.4 %fusion = f32[16,16,512]{2,0,1:T(8,128)S(1)} fusion(f32[16,16,512]{2,0,1:T(8,128)S(1)} %fusion.1, f32[16,4,512]{2,0,1:T(8,128)S(1)} %collective-permute-done.4, f32[16,4,512]{2,0,1:T(8,128)S(1)} %collective-permute-done.5, f32[24,16,520]{2,0,1:T(8,128)S(1)} %select_maximum_fusion, f32[20,24,512]{2,0,1:T(8,128)S(1)} %get-tuple-element.21, ...), kind=kOutput, calls=%fused_computation.17 | convolution fusion | flops 15993856 | bytes 10748496 | tf_op jit(solution)/shard_map/as,bs,cs->abc/dot_general | solution.py:122
  68.3 0.3 pad_maximum_fusion.4
  68.6 11.4 %slice.503 = f32[16,16,260]{2,0,1:T(8,128)S(1)} slice(f32[16,16,520]{2,0,1:T(8,128)S(1)} %pad_maximum_fusion.4), slice={[0:16:1], [0:16:1], [0:520:2]} | slice | bytes 532480 | tf_op jit(solution)/shard_map/slice | solution.py:61
  80.0 11.4 %slice.505 = f32[16,16,260]{2,0,1:T(8,128)S(1)} slice(f32[16,16,520]{2,0,1:T(8,128)S(1)} %pad_maximum_fusion.4), slice={[0:16:1], [0:16:1], [1:520:2]} | slice | bytes 532480 | tf_op jit(solution)/shard_map/slice | solution.py:62
  91.4 0.2 fusion.76
  91.6 0.3 fusion.74
  91.9 0.3 fusion.72
  92.2 0.2 multiply_bitcast_fusion.2
  92.5 0.6 copy-done.2
  93.1 0.6 copy.175
  93.7 1.0 copy.176
  94.6 1.9 %collective-permute-start.8 = (f32[4,16,512]{2,1,0:T(8,128)}, f32[4,16,512]{2,1,0:T(8,128)}, u32[]{:S(2)}, u32[]{:S(2)}) collective-permute-start(f32[4,16,512]{2,1,0:T(8,128)} %copy.176), channel_id=1, source_target_pairs={{0,1},{1,2},{2,3},{4,5},{5,6},{6,7},{8,9},{9,10},{10,11},{12,13},{... | collective-permute-start | bytes 393224 | tf_op jit(solution)/shard_map/ppermute | solution.py:21
  96.6 1.3 copy.174
  97.8 0.6 copy.179
  98.4 0.6 copy.180
  99.0 0.3 copy.181
  99.3 3.3 %collective-permute-start.9 = (f32[4,16,512]{2,1,0:T(8,128)S(1)}, f32[4,16,512]{2,1,0:T(8,128)}, u32[]{:S(2)}, u32[]{:S(2)}) collective-permute-start(f32[4,16,512]{2,1,0:T(8,128)S(1)} %copy.181), channel_id=1, source_target_pairs={{1,0},{2,1},{3,2},{5,4},{6,5},{7,6},{9,8},{10,9},{11,10},{13,12},{... | collective-permute-start | bytes 393224 | tf_op jit(solution)/shard_map/ppermute | solution.py:24
  102.6 1.0 pad_maximum_fusion.1
  103.6 4.4 %copy.178 = f32[16,16,256,2]{1,0,3,2:T(8,128)} copy(f32[16,16,256,2]{2,0,1,3:T(8,128)S(1)} %pad_maximum_fusion.1) | data formatting | bytes 1048576 | tf_op jit(solution)/shard_map/stack | solution.py:78
  108.0 3.5 %copy.184 = f32[16,16,512]{2,1,0:T(8,128)} copy(f32[16,16,512]{1,0,2:T(8,128)} %bitcast.69) | data formatting | bytes 1048576 | tf_op jit(solution)/shard_map/reshape | solution.py:80
  111.5 2.3 %copy.177 = f32[4,16,512]{1,2,0:T(8,128)} copy(f32[4,16,512]{2,1,0:T(8,128)} %collective-permute-done.8) | data formatting | bytes 262144 | tf_op jit(solution)/shard_map/ppermute | solution.py:21
  113.8 2.4 %reverse_select_fusion.1 = f32[4,16,512]{1,2,0:T(8,128)} fusion(f32[4,16,512]{1,2,0:T(8,128)} %copy.177, f32[4,16,512]{1,2,0:T(8,128)S(1)} %bitcast.75, pred[]{:T(512)S(6)} %eq.215), kind=kLoop, calls=%fused_computation.29 | loop fusion | flops 32768 | bytes 393217 | tf_op jit(solution)/shard_map/jit(_where)/select_n | solution.py:91
  116.2 1.5 %copy.183 = f32[4,16,512]{2,1,0:T(8,128)S(1)} copy(f32[4,16,512]{1,2,0:T(8,128)} %reverse_select_fusion.1) | data formatting | bytes 262144 | tf_op jit(solution)/shard_map/jit(_where)/select_n | solution.py:91
  117.7 1.2 copy.182
  119.0 1.1 reverse_select_fusion
  120.0 1.6 %copy.185 = f32[4,16,512]{2,1,0:T(8,128)S(1)} copy(f32[4,16,512]{1,2,0:T(8,128)} %reverse_select_fusion) | data formatting | bytes 262144 | tf_op jit(solution)/shard_map/jit(_where)/select_n | solution.py:94
  122.2 4.1 %collective-permute-start.10 = (f32[16,4,512]{2,1,0:T(4,128)S(1)}, f32[16,4,512]{2,1,0:T(4,128)S(1)}, u32[]{:S(2)}, u32[]{:S(2)}) collective-permute-start(f32[16,4,512]{2,1,0:T(4,128)S(1)} %get-tuple-element.28), channel_id=1, source_target_pairs={{0,4},{4,8},{8,12},{1,5},{5,9},{9,13},{2,6},{6,10},{10,14},{3,7},{... | collective-permute-start | bytes 393224 | tf_op jit(solution)/shard_map/ppermute | solution.py:21
  126.3 1.1 copy.190
  127.4 1.1 copy.189
  128.5 0.2 rev.28
  128.8 0.3 rev.27
  129.0 1.3 collective-permute-start.11
  130.4 4.7 %collective-permute-done.11 = f32[16,4,512]{2,1,0:T(4,128)S(1)} collective-permute-done((f32[16,4,512]{2,1,0:T(4,128)S(1)}, f32[16,4,512]{2,1,0:T(4,128)S(1)}, u32[]{:S(2)}, u32[]{:S(2)}) %collective-permute-start.11) | collective-permute-done | bytes 131104 | tf_op jit(solution)/shard_map/ppermute | solution.py:24
  135.2 0.2 slice.543
  135.5 0.2 slice.545
  136.3 0.2 multiply_multiply_fusion
  136.5 0.3 copy.188
  136.8 1.1 copy.191
  (50 shorter events, 2.2 us)
Async XLA Ops:
  0.6 8.0 %copy-start = (f32[256]{0:T(256)S(1)}, f32[256]{0:T(256)}, u32[]{:S(2)}) copy-start(f32[256]{0:T(256)} %param.11) | copy-start | bytes 3076
  0.6 10.1 %copy-start.4 = (f32[16,16,512]{2,1,0:T(8,128)S(1)}, f32[16,16,512]{2,1,0:T(8,128)}, u32[]{:S(2)}) copy-start(f32[16,16,512]{2,1,0:T(8,128)} %param.7) | copy-start | bytes 1572868
  0.7 9.4 %copy-start.5 = (f32[16]{0:T(128)S(1)}, f32[16]{0:T(128)}, u32[]{:S(2)}) copy-start(f32[16]{0:T(128)} %param.10) | copy-start | bytes 196
  1.9 8.8 %collective-permute-start = (f32[16,4,512]{2,0,1:T(8,128)S(1)}, f32[16,4,512]{2,0,1:T(8,128)S(1)}, u32[]{:S(2)}, u32[]{:S(2)}) collective-permute-start(f32[16,4,512]{2,0,1:T(8,128)S(1)} %copy.205), channel_id=1, source_target_pairs={{0,4},{4,8},{8,12},{1,5},{5,9},{9,13},{2,6},{6,10},{10,14},{3,7},{... | collective-permute-start | bytes 393224 | tf_op jit(solution)/shard_map/ppermute | solution.py:21
  6.0 5.7 %collective-permute-start.1 = (f32[16,4,512]{2,0,1:T(8,128)S(1)}, f32[16,4,512]{2,0,1:T(8,128)S(1)}, u32[]{:S(2)}, u32[]{:S(2)}) collective-permute-start(f32[16,4,512]{2,0,1:T(8,128)S(1)} %copy.206), channel_id=1, source_target_pairs={{4,0},{8,4},{12,8},{5,1},{9,5},{13,9},{6,2},{10,6},{14,10},{7,3},{... | collective-permute-start | bytes 393224 | tf_op jit(solution)/shard_map/ppermute | solution.py:24
  11.8 10.3 %copy-start.6 = (f32[16,16,512]{2,1,0:T(8,128)S(1)}, f32[16,16,512]{2,1,0:T(8,128)}, u32[]{:S(2)}) copy-start(f32[16,16,512]{2,1,0:T(8,128)} %param.8) | copy-start | bytes 1572868
  11.8 10.3 %copy-start.7 = (s32[16,16,512]{2,1,0:T(8,128)S(1)}, s32[16,16,512]{2,1,0:T(8,128)}, u32[]{:S(2)}) copy-start(s32[16,16,512]{2,1,0:T(8,128)} %param.9) | copy-start | bytes 1572868
  11.8 8.6 %collective-permute-start.2 = (f32[4,24,512]{2,0,1:T(4,128)S(1)}, f32[4,24,512]{2,0,1:T(4,128)S(1)}, u32[]{:S(2)}, u32[]{:S(2)}) collective-permute-start(f32[4,24,512]{2,0,1:T(4,128)S(1)} %get-tuple-element.24), channel_id=1, source_target_pairs={{1,0},{2,1},{3,2},{5,4},{6,5},{7,6},{9,8},{10,9},{11,10},{13,12},{... | collective-permute-start | bytes 589832 | tf_op jit(solution)/shard_map/ppermute | solution.py:24
  16.0 5.6 %collective-permute-start.3 = (f32[4,24,512]{2,0,1:T(4,128)S(1)}, f32[4,24,512]{2,0,1:T(4,128)S(1)}, u32[]{:S(2)}, u32[]{:S(2)}) collective-permute-start(f32[4,24,512]{2,0,1:T(4,128)S(1)} %get-tuple-element.25), channel_id=1, source_target_pairs={{0,1},{1,2},{2,3},{4,5},{5,6},{6,7},{8,9},{9,10},{10,11},{12,13},{... | collective-permute-start | bytes 589832 | tf_op jit(solution)/shard_map/ppermute | solution.py:21
  35.1 5.7 %collective-permute-start.5 = (f32[16,4,512]{2,0,1:T(8,128)S(1)}, f32[16,4,512]{2,0,1:T(8,128)S(1)}, u32[]{:S(2)}, u32[]{:S(2)}) collective-permute-start(f32[16,4,512]{2,0,1:T(8,128)S(1)} %get-tuple-element.38), channel_id=1, source_target_pairs={{4,0},{8,4},{12,8},{5,1},{9,5},{13,9},{6,2},{10,6},{14,10},{7,3},{... | collective-permute-start | bytes 393224 | tf_op jit(solution)/shard_map/ppermute | solution.py:24
  36.4 5.9 %collective-permute-start.4 = (f32[16,4,512]{2,0,1:T(8,128)S(1)}, f32[16,4,512]{2,0,1:T(8,128)S(1)}, u32[]{:S(2)}, u32[]{:S(2)}) collective-permute-start(f32[16,4,512]{2,0,1:T(8,128)S(1)} %get-tuple-element.39), channel_id=1, source_target_pairs={{0,4},{4,8},{8,12},{1,5},{5,9},{9,13},{2,6},{6,10},{10,14},{3,7},{... | collective-permute-start | bytes 393224 | tf_op jit(solution)/shard_map/ppermute | solution.py:21
  42.4 8.1 %collective-permute-start.7 = (f32[4,24,512]{2,0,1:T(4,128)S(1)}, f32[4,24,512]{2,0,1:T(4,128)S(1)}, u32[]{:S(2)}, u32[]{:S(2)}) collective-permute-start(f32[4,24,512]{2,0,1:T(4,128)S(1)} %get-tuple-element.22), channel_id=1, source_target_pairs={{0,1},{1,2},{2,3},{4,5},{5,6},{6,7},{8,9},{9,10},{10,11},{12,13},{... | collective-permute-start | bytes 589832 | tf_op jit(solution)/shard_map/ppermute | solution.py:21
  47.9 7.0 %collective-permute-start.6 = (f32[4,24,512]{2,0,1:T(4,128)S(1)}, f32[4,24,512]{2,0,1:T(4,128)S(1)}, u32[]{:S(2)}, u32[]{:S(2)}) collective-permute-start(f32[4,24,512]{2,0,1:T(4,128)S(1)} %get-tuple-element.23), channel_id=1, source_target_pairs={{1,0},{2,1},{3,2},{5,4},{6,5},{7,6},{9,8},{10,9},{11,10},{13,12},{... | collective-permute-start | bytes 589832 | tf_op jit(solution)/shard_map/ppermute | solution.py:24
  92.4 0.7 copy-start.2
  94.6 16.8 %collective-permute-start.8 = (f32[4,16,512]{2,1,0:T(8,128)}, f32[4,16,512]{2,1,0:T(8,128)}, u32[]{:S(2)}, u32[]{:S(2)}) collective-permute-start(f32[4,16,512]{2,1,0:T(8,128)} %copy.176), channel_id=1, source_target_pairs={{0,1},{1,2},{2,3},{4,5},{5,6},{6,7},{8,9},{9,10},{10,11},{12,13},{... | collective-permute-start | bytes 393224 | tf_op jit(solution)/shard_map/ppermute | solution.py:21
  99.3 18.4 %collective-permute-start.9 = (f32[4,16,512]{2,1,0:T(8,128)S(1)}, f32[4,16,512]{2,1,0:T(8,128)}, u32[]{:S(2)}, u32[]{:S(2)}) collective-permute-start(f32[4,16,512]{2,1,0:T(8,128)S(1)} %copy.181), channel_id=1, source_target_pairs={{1,0},{2,1},{3,2},{5,4},{6,5},{7,6},{9,8},{10,9},{11,10},{13,12},{... | collective-permute-start | bytes 393224 | tf_op jit(solution)/shard_map/ppermute | solution.py:24
  111.5 2.3 %copy-start.1 = (f32[4,16,256,2]{1,3,2,0:T(2,128)S(1)}, f32[4,16,256,2]{1,3,2,0:T(2,128)}, u32[]{:S(2)}) copy-start(f32[4,16,256,2]{1,3,2,0:T(2,128)} %copy.174) | copy-start | bytes 393220
  120.0 1.6 %copy-start.3 = (f32[16,16,512]{2,1,0:T(8,128)S(1)}, f32[16,16,512]{2,1,0:T(8,128)}, u32[]{:S(2)}) copy-start(f32[16,16,512]{2,1,0:T(8,128)} %copy.184) | copy-start | bytes 1572868
  122.2 8.1 %collective-permute-start.10 = (f32[16,4,512]{2,1,0:T(4,128)S(1)}, f32[16,4,512]{2,1,0:T(4,128)S(1)}, u32[]{:S(2)}, u32[]{:S(2)}) collective-permute-start(f32[16,4,512]{2,1,0:T(4,128)S(1)} %get-tuple-element.28), channel_id=1, source_target_pairs={{0,4},{4,8},{8,12},{1,5},{5,9},{9,13},{2,6},{6,10},{10,14},{3,7},{... | collective-permute-start | bytes 393224 | tf_op jit(solution)/shard_map/ppermute | solution.py:21
  129.0 6.0 %collective-permute-start.11 = (f32[16,4,512]{2,1,0:T(4,128)S(1)}, f32[16,4,512]{2,1,0:T(4,128)S(1)}, u32[]{:S(2)}, u32[]{:S(2)}) collective-permute-start(f32[16,4,512]{2,1,0:T(4,128)S(1)} %get-tuple-element.29), channel_id=1, source_target_pairs={{4,0},{8,4},{12,8},{5,1},{9,5},{13,9},{6,2},{10,6},{14,10},{7,3},{... | collective-permute-start | bytes 393224 | tf_op jit(solution)/shard_map/ppermute | solution.py:24
where the time goes:
time: 139 us; the launch traced here: 138 us
  local copies, waits for them, and re-layouts  50.9 us (37%)
  starting transfers between devices  35.9 us (26%)
  matrix products  25.3 us (18%)
  waiting for transfers between devices  14.6 us (11%)
  other arithmetic  9.95 us (7%)
    dot_general x2, matrix products, source_block(): jnp.einsum('as,bs,cs->abc', match_x, match_y * amplitude[None, :], match_...  25.3 us
    ppermute x6, starting transfers between devices, padded_2(): lax.ppermute(lax.slice_in_dim(block, block.shape[dim] - width, None, axis...  22.6 us
    ppermute x6, starting transfers between devices, padded_2(): lax.ppermute(lax.slice_in_dim(block, 0, width, axis=dim), axis, backward)  13.4 us
    slice x3, local copies, waits for them, and re-layouts, lift_core(): odd = lax.slice_in_dim(padded, 1, length, 2, along)  11.7 us
    slice x2, local copies, waits for them, and re-layouts, lift_core(): even = lax.slice_in_dim(padded, 0, length, 2, along)  11.6 us
    ppermute x6, waiting for transfers between devices, padded_2(): lax.ppermute(lax.slice_in_dim(block, 0, width, axis=dim), axis, backward)  11.4 us
    unnamed x23, local copies, waits for them, and re-layouts  4.39 us
    another operation x1, local copies, waits for them, and re-layouts, lift_core(): joined = jnp.stack([low_band, high_band], along + 1)  4.37 us
  transfers between devices with their start and end apart: 12, of which 8 were waited for; matrix products, arithmetic and copies ran while one was open for 18% of the time, Pallas kernels for 0%

commit v1 on v0

v1 whole, which is shorter than its diff:
```python
import functools

import jax
import jax.numpy as jnp
import ml_dtypes
import numpy as np
from jax import lax
from jax.experimental import pallas as pl
from jax.experimental.pallas import tpu as pltpu
from jax.sharding import PartitionSpec as P

STENCIL_WEIGHTS = (-205.0 / 72.0, 8.0 / 5.0, -1.0 / 5.0, 8.0 / 315.0, -1.0 / 560.0)
LIFT_ALPHA = -1.586134342
LIFT_BETA = -0.05298011854
LIFT_GAMMA = 0.8829110762
LIFT_DELTA = 0.4435068522
LIFT_SCALE = 1.149604398
DEAD_ZONE = 0.25
QUANT_STEP = 0.5
W = 4
MESH = pl.DeviceIdType.MESH


def lift_matrix(size):
    field = np.eye(size + 2 * W)
    even, odd = field[0::2], field[1::2]
    odd = odd[:-1] + LIFT_ALPHA * (even[:-1] + even[1:])
    even = even[1:-1] + LIFT_BETA * (odd[:-1] + odd[1:])
    odd = odd[1:-1] + LIFT_GAMMA * (even[:-1] + even[1:])
    even = even[1:-1] + LIFT_DELTA * (odd[:-1] + odd[1:])
    out = np.zeros((size, size + 2 * W))
    out[0::2] = even / LIFT_SCALE
    out[1::2] = odd[1:] * LIFT_SCALE
    return out


def reflected(matrix, first, last):
    size = matrix.shape[0]
    out = matrix.copy()
    for step in range(1, W + 1):
        if first:
            out[:, W + step] += out[:, W - step]
            out[:, W - step] = 0.0
        if last:
            out[:, W + size - 1 - step] += out[:, W + size - 1 + step]
            out[:, W + size - 1 + step] = 0.0
    return out


def halves(matrix):
    wide = np.asarray(matrix, np.float32)
    high = wide.astype(ml_dtypes.bfloat16)
    low = (wide - high.astype(np.float32)).astype(ml_dtypes.bfloat16)
    return np.stack([high, low], axis=-3)


def halo_cells(rows_x, rows_y):
    low, x_high, y_high = range(-W, 0), range(rows_x, rows_x + W), range(rows_y, rows_y + W)
    cells = [(x, y) for x in low for y in range(rows_y)]
    cells += [(x, y) for x in x_high for y in range(rows_y)]
    cells += [(x, y) for x in range(rows_x) for y in low]
    cells += [(x, y) for x in range(rows_x) for y in y_high]
    faces = len(cells)
    for side_x in (low, x_high):
        for side_y in (low, y_high):
            cells += [(x, y) for x in side_x for y in side_y]
    return cells, faces


@functools.lru_cache(None)
def tables(rows_x, rows_y, depth):
    cells, faces = halo_cells(rows_x, rows_y)
    own = [(x, y) for x in range(rows_x) for y in range(rows_y)]
    everywhere = np.array(own + cells)
    target = np.array(own)
    gap_x = np.abs(target[:, None, 0] - everywhere[None, :, 0])
    gap_y = np.abs(target[:, None, 1] - everywhere[None, :, 1])
    weights = np.array(list(STENCIL_WEIGHTS) + [0.0])
    star = np.where(gap_y == 0, weights[np.minimum(gap_x, W + 1)], 0.0)
    star = star + np.where(gap_x == 0, weights[np.minimum(gap_y, W + 1)], 0.0)
    star = star[:, : len(own) + faces]
    spot = np.arange(depth)
    along = weights[np.minimum(np.abs(spot[:, None] - spot[None, :]), W + 1)]
    depth_lift = reflected(lift_matrix(depth), True, True)[:, W : W + depth].T
    kinds = ((False, False), (True, False), (False, True))
    lifts = []
    for kind_x in kinds:
        for kind_y in kinds:
            by_x = reflected(lift_matrix(rows_x), *kind_x)[:, everywhere[:, 0] + W]
            by_y = reflected(lift_matrix(rows_y), *kind_y)[:, everywhere[:, 1] + W]
            lifts.append(by_x[target[:, 0]] * by_y[target[:, 1]])
    lifts = np.stack(lifts)
    spare = -lifts.shape[2] % 128
    lifts = np.pad(lifts, ((0, 0), (0, 0), (0, spare)))
    depth_both = np.concatenate([halves(along), halves(depth_lift)])
    return halves(star), depth_both, halves(lifts)


def split(values):
    high = values.astype(jnp.bfloat16)
    return high, (values - high.astype(jnp.float32)).astype(jnp.bfloat16)


def product(left, right):
    dot = functools.partial(jnp.dot, preferred_element_type=jnp.float32)
    return dot(left[0], right[0]) + (dot(left[0], right[1]) + dot(left[1], right[0]))


def choose(classes, entries, bit):
    if len(entries) == 1:
        return entries[0]
    half = len(entries) // 2
    low = choose(classes, entries[:half], bit // 2)
    high = choose(classes, entries[half:], bit // 2)
    return jnp.where((classes & bit) != 0, high, low)


def kernel(
    rows_x, rows_y,
    cells_ref, samples_ref, wave_ref, table_ref,
    now_hbm, old_hbm, classes_hbm, star_hbm, along_hbm, lift_hbm,
    next_hbm, mid_hbm, code_hbm,
    now, old, classes, star, along, lift,
    courant, mid, later, acc, packed, halo_a, halo_b, halo_c,
    local_sem, out_sem, send_sem, recv_sem,
):
    depth = now.shape[1]
    size = rows_x * rows_y
    face_x, face_y, corner = W * rows_y, W * rows_x, W * W
    faces = 2 * face_x + 2 * face_y
    at_x, at_y = lax.axis_index("gx"), lax.axis_index("gy")
    count_x, count_y = lax.axis_size("gx"), lax.axis_size("gy")
    shot = lax.axis_index("shot")
    low_x, high_x = at_x > 0, at_x < count_x - 1
    low_y, high_y = at_y > 0, at_y < count_y - 1
    kind_x = jnp.where(low_x, jnp.where(high_x, 0, 2), 1)
    kind_y = jnp.where(low_y, jnp.where(high_y, 0, 2), 1)

    pulls = [
        pltpu.make_async_copy(src, dst, local_sem.at[i])
        for i, (src, dst) in enumerate(
            [
                (now_hbm, now), (classes_hbm, classes), (old_hbm, old),
                (star_hbm, star), (along_hbm, along),
                (lift_hbm.at[kind_x * 3 + kind_y], lift),
            ]
        )
    ]
    for pull in pulls:
        pull.start()

    steps = ((-1, low_x, low_y), (1, high_x, high_y))
    partners = [(dx, 0, has) for dx, has, _ in steps] + [(0, dy, has) for dy, _, has in steps]
    partners += [
        (dx, dy, jnp.logical_and(has_x, has_y)) for dx, has_x, _ in steps for dy, _, has_y in steps
    ]

    def device(dx, dy):
        return {"shot": shot, "gy": at_y + dy, "gx": at_x + dx}

    barrier = pltpu.get_barrier_semaphore()
    for dx, dy, has in partners:
        @pl.when(has)
        def _(dx=dx, dy=dy):
            pl.semaphore_signal(barrier, inc=1, device_id=device(dx, dy), device_id_type=MESH)

    def pack(source, where):
        for x in range(0, rows_x, 2):
            first, second = x * rows_y, (x + 1) * rows_y
            packed[where, 0, x * W : (x + 2) * W, :] = jnp.concatenate(
                [source[first : first + W, :], source[second : second + W, :]], axis=0
            )
            packed[where, 1, x * W : (x + 2) * W, :] = jnp.concatenate(
                [source[first + rows_y - W : second, :],
                 source[second + rows_y - W : second + rows_y, :]], axis=0
            )

    slots = [(0, face_x), (face_x, face_x), (2 * face_x, face_y), (2 * face_x + face_y, face_y)]
    slots += [(faces + i * corner, corner) for i in range(4)]

    def exchange(source, halo, where, base, with_corners):
        ends = [
            source.at[pl.ds(0, face_x)],
            source.at[pl.ds(size - face_x, face_x)],
            packed.at[where, 0],
            packed.at[where, 1],
            packed.at[where, 0, pl.ds(0, corner)],
            packed.at[where, 1, pl.ds(0, corner)],
            packed.at[where, 0, pl.ds(face_y - corner, corner)],
            packed.at[where, 1, pl.ds(face_y - corner, corner)],
        ]
        opposite = [1, 0, 3, 2, 7, 6, 5, 4]
        sends, arrivals = [], []
        for i in range(8 if with_corners else 4):
            dx, dy, has = partners[i]
            for to, found in ((opposite[i], sends), (i, arrivals)):
                start, length = slots[to]
                found.append((has, pltpu.make_async_remote_copy(
                    src_ref=ends[i],
                    dst_ref=halo.at[pl.ds(start, length)],
                    send_sem=send_sem.at[base + i],
                    recv_sem=recv_sem.at[base + to],
                    device_id=device(dx, dy),
                    device_id_type=MESH,
                )))
        return sends, arrivals

    def each(copies, act):
        for has, copy in copies:
            @pl.when(has)
            def _(copy=copy):
                act(copy)

    start = lambda copy: copy.start()
    landed = lambda copy: copy.wait_recv()
    sent = lambda copy: copy.wait_send()

    first_sends, first_lands = exchange(now, halo_a, 0, 0, False)
    second_sends, second_lands = exchange(mid, halo_b, 1, 4, False)
    third_sends, third_lands = exchange(later, halo_c, 2, 8, True)

    for halo, lands in ((halo_a, first_lands), (halo_b, second_lands), (halo_c, third_lands)):
        for i, (has, _) in enumerate(lands):
            begin, length = slots[i]

            @pl.when(jnp.logical_not(has))
            def _(halo=halo, begin=begin, length=length):
                halo[begin : begin + length, :] = jnp.zeros((length, depth), jnp.float32)
    tail = faces + 4 * corner
    if halo_c.shape[0] > tail:
        halo_c[tail:, :] = jnp.zeros((halo_c.shape[0] - tail, depth), jnp.float32)

    pulls[0].wait()
    pack(now, 0)
    near_x = low_x.astype(jnp.int32) + high_x.astype(jnp.int32)
    near_y = low_y.astype(jnp.int32) + high_y.astype(jnp.int32)
    pl.semaphore_wait(barrier, near_x + near_y + near_x * near_y)
    each(first_sends[2:], start)
    each(first_sends[:2], start)

    wave_len = wave_ref.shape[0]
    all_y = rows_y * count_y
    shots = []
    for s in range(cells_ref.shape[0]):
        cell, sample = cells_ref[s], samples_ref[s]
        cell_x = lax.div(cell, all_y * depth) - at_x * rows_x
        cell_y = lax.rem(lax.div(cell, depth), all_y) - at_y * rows_y
        here = (cell_x >= 0) & (cell_x < rows_x) & (cell_y >= 0) & (cell_y < rows_y)
        spot = jnp.where(here, (cell_x * rows_y + cell_y) * depth + lax.rem(cell, depth), -1)
        following = jnp.where(sample + 1 >= wave_len, 0, sample + 1)
        shots.append((spot, wave_ref[sample], wave_ref[following]))
    entries = [table_ref[i] for i in range(table_ref.shape[0])]
    while len(entries) & (len(entries) - 1):
        entries.append(entries[-1])
    pulls[1].wait()
    pulls[2].wait()

    def plane(x, carry):
        rows = pl.ds(pl.multiple_of(x * rows_y, rows_y), rows_y)
        courant[rows, :] = jnp.broadcast_to(
            choose(classes[rows, :], entries, len(entries) // 2), (rows_y, depth)
        )
        place = lax.broadcasted_iota(jnp.int32, (rows_y, depth), 0) * depth
        place = place + lax.broadcasted_iota(jnp.int32, (rows_y, depth), 1)
        here = now[rows, :]
        base_a = 2.0 * here - old[rows, :]
        base_b = -here
        for spot, amp_a, amp_b in shots:
            hit = place == spot - x * (rows_y * depth)
            base_a = base_a + jnp.where(hit, amp_a, 0.0)
            base_b = base_b + jnp.where(hit, amp_b, 0.0)
        old[rows, :] = base_a
        later[rows, :] = base_b
        return carry

    lax.fori_loop(0, rows_x, plane, 0)
    pulls[3].wait()
    pulls[4].wait()

    def inner(field):
        both = split(field[...])
        own = [star[0, :, :size], star[1, :, :size]]
        acc[...] = product(own, both) + product(both, (along[0], along[1]))

    def outer(halo):
        return product([star[0, :, size:], star[1, :, size:]], split(halo[...]))

    inner(now)
    each(first_lands, landed)
    mid[...] = old[...] + courant[...] * (acc[...] + outer(halo_a))
    each(second_sends[:2], start)
    pack(mid, 1)
    each(second_sends[2:], start)
    mid_out = pltpu.make_async_copy(mid, mid_hbm, out_sem.at[0])
    mid_out.start()

    later[...] = later[...] + 2.0 * mid[...]
    inner(mid)
    each(second_lands, landed)
    later[...] = later[...] + courant[...] * (acc[...] + outer(halo_b))
    each(third_sends[:2], start)
    pack(later, 2)
    each(third_sends[2:], start)
    next_out = pltpu.make_async_copy(later, next_hbm, out_sem.at[1])
    next_out.start()

    pulls[5].wait()
    acc[...] = product([lift[0, :, :size], lift[1, :, :size]], split(later[...]))
    each(third_lands, landed)
    lifted = acc[...] + product([lift[0, :, size:], lift[1, :, size:]], split(halo_c[...]))
    lifted = product(split(lifted), (along[2], along[3]))
    shrunk = jnp.maximum(jnp.abs(lifted) - DEAD_ZONE, 0.0) / QUANT_STEP
    acc[...] = jnp.where(lifted < 0.0, -shrunk, shrunk)
    code_out = pltpu.make_async_copy(acc, code_hbm, out_sem.at[2])
    code_out.start()
    each(first_sends, sent)
    each(second_sends, sent)
    each(third_sends, sent)
    mid_out.wait()
    next_out.wait()
    code_out.wait()


def shards(pressure_now, pressure_old, classes, class_table, wavelet, source_cells, samples):
    rows_x, rows_y, depth = pressure_now.shape
    size = rows_x * rows_y
    flat = (size, depth)
    star, along, lift = tables(rows_x, rows_y, depth)
    halo_rows = star.shape[2] - size
    wide_rows = lift.shape[3] - size
    face_y = W * rows_x
    any_spec = pl.BlockSpec(memory_space=pl.ANY)
    smem = pl.BlockSpec(memory_space=pltpu.SMEM)
    f32 = jnp.float32
    out = jax.ShapeDtypeStruct(flat, f32)
    results = pl.pallas_call(
        functools.partial(kernel, rows_x, rows_y),
        out_shape=(out, out, out),
        in_specs=[smem] * 4 + [any_spec] * 6,
        out_specs=(any_spec,) * 3,
        scratch_shapes=[
            pltpu.VMEM(flat, f32),
            pltpu.VMEM(flat, f32),
            pltpu.VMEM(flat, jnp.int32),
            pltpu.VMEM(star.shape, jnp.bfloat16),
            pltpu.VMEM(along.shape, jnp.bfloat16),
            pltpu.VMEM(lift.shape[1:], jnp.bfloat16),
            pltpu.VMEM(flat, f32),
            pltpu.VMEM(flat, f32),
            pltpu.VMEM(flat, f32),
            pltpu.VMEM(flat, f32),
            pltpu.VMEM((3, 2, face_y, depth), f32),
            pltpu.VMEM((halo_rows, depth), f32),
            pltpu.VMEM((halo_rows, depth), f32),
            pltpu.VMEM((wide_rows, depth), f32),
            pltpu.SemaphoreType.DMA((6,)),
            pltpu.SemaphoreType.DMA((3,)),
            pltpu.SemaphoreType.DMA((16,)),
            pltpu.SemaphoreType.DMA((16,)),
        ],
        compiler_params=pltpu.CompilerParams(
            collective_id=0, has_side_effects=True, vmem_limit_bytes=40 * 1024 * 1024
        ),
    )(
        source_cells, samples, wavelet, class_table,
        pressure_now.reshape(flat), pressure_old.reshape(flat), classes.reshape(flat),
        jnp.asarray(star), jnp.asarray(along), jnp.asarray(lift),
    )
    return tuple(result.reshape(pressure_now.shape) for result in results)


def solution(mesh):
    block = P(("shot", "gx"), "gy", None)
    return jax.shard_map(
        shards,
        mesh=mesh,
        in_specs=(block, block, block, P(), P("shot"), P("shot"), P("shot")),
        out_specs=(block, block, block),
        check_vma=False,
    )
```

time: 139 us -> 36.8 us (0.26)
  local copies, waits for them, and re-layouts: 50.9 us -> 13.4 us
  starting transfers between devices: 35.9 us -> 0 us
  matrix products: 25.3 us -> 0 us
  Pallas kernels: 0 us -> 22.1 us
  waiting for transfers between devices: 14.6 us -> 0 us
  other arithmetic: 9.95 us -> 0 us
    ppermute x12 -> x0, starting transfers between devices: 35.9 us -> none  [the longest x6 22.6 us: padded_2(): lax.ppermute(lax.slice_in_dim(block, block.shape[dim] - width, None, axis...]
    slice x17 -> x0, local copies, waits for them, and re-layouts: 29.7 us -> none  [the longest x3 11.7 us: lift_core(): odd = lax.slice_in_dim(padded, 1, length, 2, along)]
    dot_general x2 -> x0, matrix products: 25.3 us -> none  [source_block(): jnp.einsum('as,bs,cs->abc', match_x, match_y * amplitude[None, :], match_...]
    pallas_call x0 -> x1, Pallas kernels: none -> 22.1 us  [shards(): pl.pallas_call(functools.partial(kernel, rows_x, rows_y), out_shape=(out,...]
    ppermute x12 -> x0, waiting for transfers between devices: 14.6 us -> none  [the longest x6 11.4 us: padded_2(): lax.ppermute(lax.slice_in_dim(block, 0, width, axis=dim), axis, backward)]
    unnamed x23, local copies, waits for them, and re-layouts: 4.39 us -> 13.4 us
    select_n x6 -> x0, other arithmetic: 4.87 us -> none  [the longest x2 2.42 us: mend_edges(): jnp.where(at_first, jnp.flip(cut_range(field, 1, 5, along), along), cut_r...]
    another operation x1 -> x0, local copies, waits for them, and re-layouts: 4.37 us -> none  [lift_core(): joined = jnp.stack([low_band, high_band], along + 1)]
  transfers between devices with their start and end apart: 12 -> 0, of which waited for: 8 -> 0; matrix products, arithmetic and copies ran while one was open for 18% -> 0% of each run, Pallas kernels for 0% -> 0%
where the time goes in v1:
time: 36.8 us; the launch traced here: 36.2 us
  Pallas kernels  22.1 us (60%)
  local copies, waits for them, and re-layouts  13.4 us (36%)
  between operations  0.66 us (2%)
    pallas_call x1, Pallas kernels, shards(): pl.pallas_call(functools.partial(kernel, rows_x, rows_y), out_shape=(out,...  22.1 us
    unnamed x23, local copies, waits for them, and re-layouts  13.4 us

profile of v1, /device:TPU:1, one launch (start us, length us, event | category | flops | bytes accessed | tf_op | source)
XLA Modules:
  0.0 36.2 jit_solution(11012224072917532012)
XLA Ops:
  0.6 0.0 copy-start
  0.6 2.7 %copy-done = bf16[9,2,256,640]{3,2,1,0:T(8,128)(2,1)S(1)} copy-done((bf16[9,2,256,640]{3,2,1,0:T(8,128)(2,1)S(1)}, bf16[9,2,256,640]{3,2,1,0:T(8,128)(2,1)}, u32[]{:S(2)}) %copy-start) | copy-done | bytes 5898264
  3.3 0.0 copy-start.1
  3.3 1.6 %copy-done.1 = bf16[4,512,512]{2,1,0:T(8,128)(2,1)S(1)} copy-done((bf16[4,512,512]{2,1,0:T(8,128)(2,1)S(1)}, bf16[4,512,512]{2,1,0:T(8,128)(2,1)}, u32[]{:S(2)}) %copy-start.1) | copy-done | bytes 2097176
  4.9 0.0 copy-start.2
  4.9 1.0 %copy-done.2 = f32[16,16,512]{2,1,0:T(8,128)S(1)} copy-done((f32[16,16,512]{2,1,0:T(8,128)S(1)}, f32[16,16,512]{2,1,0:T(8,128)}, u32[]{:S(2)}) %copy-start.2) | copy-done | bytes 524312
  5.9 0.0 copy-start.3
  5.9 1.0 %copy-done.3 = f32[16,16,512]{2,1,0:T(8,128)S(1)} copy-done((f32[16,16,512]{2,1,0:T(8,128)S(1)}, f32[16,16,512]{2,1,0:T(8,128)}, u32[]{:S(2)}) %copy-start.3) | copy-done | bytes 524312
  7.0 0.0 copy-start.4
  7.0 1.0 %copy-done.4 = s32[16,16,512]{2,1,0:T(8,128)S(1)} copy-done((s32[16,16,512]{2,1,0:T(8,128)S(1)}, s32[16,16,512]{2,1,0:T(8,128)}, u32[]{:S(2)}) %copy-start.4) | copy-done | bytes 524312
  8.0 0.0 copy-start.5
  8.0 1.0 %copy-done.5 = bf16[2,256,512]{2,1,0:T(8,128)(2,1)S(1)} copy-done((bf16[2,256,512]{2,1,0:T(8,128)(2,1)S(1)}, bf16[2,256,512]{2,1,0:T(8,128)(2,1)}, u32[]{:S(2)}) %copy-start.5) | copy-done | bytes 524312
  9.1 0.0 copy-start.6
  9.1 0.7 %copy-done.6 = f32[256]{0:T(256)S(1)} copy-done((f32[256]{0:T(256)S(1)}, f32[256]{0:T(256)}, u32[]{:S(2)}) %copy-start.6) | copy-done | bytes 1048
  9.7 0.0 copy-start.7
  9.8 0.7 %copy-done.7 = s32[4]{0:T(128)S(1)} copy-done((s32[4]{0:T(128)S(1)}, s32[4]{0:T(128)}, u32[]{:S(2)}) %copy-start.7) | copy-done | bytes 40
  10.4 0.0 copy-start.8
  10.4 0.7 %copy-done.8 = s32[4]{0:T(128)S(1)} copy-done((s32[4]{0:T(128)S(1)}, s32[4]{0:T(128)}, u32[]{:S(2)}) %copy-start.8) | copy-done | bytes 40
  11.1 0.0 copy-start.9
  11.1 0.7 %copy-done.9 = f32[16]{0:T(128)S(1)} copy-done((f32[16]{0:T(128)S(1)}, f32[16]{0:T(128)}, u32[]{:S(2)}) %copy-start.9) | copy-done | bytes 88
  11.7 22.1 %shard_map.121 = (f32[256,512]{1,0:T(8,128)S(1)}, f32[256,512]{1,0:T(8,128)S(1)}, f32[256,512]{1,0:T(8,128)S(1)}) custom-call(s32[4]{0:T(128)S(1)} %copy-done.7, s32[4]{0:T(128)S(1)} %copy-done.8, f32[256]{0:T(256)S(1)} %copy-done.6, f32[16]{0:T(128)S(1)} %copy-done.9, f32[256,512]{1,0:T(8,128)S(1)} %bitcast.6, f32[256,512]{1,0:T(8,128)S(1)} %bitcast.7, ...), custom_call_target="tpu_custom_call" | custom-call | tf_op jit(solution)/shard_map/pallas_call | solution.py:336
  33.8 0.8 %copy.16 = f32[16,16,512]{2,1,0:T(8,128)} copy(f32[16,16,512]{2,1,0:T(8,128)S(1)} %bitcast.11) | data formatting | bytes 1048576
  34.6 0.8 %copy.17 = f32[16,16,512]{2,1,0:T(8,128)} copy(f32[16,16,512]{2,1,0:T(8,128)S(1)} %bitcast.10) | data formatting | bytes 1048576
  35.4 0.8 %copy.18 = f32[16,16,512]{2,1,0:T(8,128)} copy(f32[16,16,512]{2,1,0:T(8,128)S(1)} %bitcast.9) | data formatting | bytes 1048576
Async XLA Ops:
  0.6 2.7 %copy-start = (bf16[9,2,256,640]{3,2,1,0:T(8,128)(2,1)S(1)}, bf16[9,2,256,640]{3,2,1,0:T(8,128)(2,1)}, u32[]{:S(2)}) copy-start(bf16[9,2,256,640]{3,2,1,0:T(8,128)(2,1)} %constant.8.clone.lift_hbm) | copy-start | bytes 17694724
  3.3 1.6 %copy-start.1 = (bf16[4,512,512]{2,1,0:T(8,128)(2,1)S(1)}, bf16[4,512,512]{2,1,0:T(8,128)(2,1)}, u32[]{:S(2)}) copy-start(bf16[4,512,512]{2,1,0:T(8,128)(2,1)} %constant.7.clone.along_hbm) | copy-start | bytes 6291460
  4.9 1.0 %copy-start.2 = (f32[16,16,512]{2,1,0:T(8,128)S(1)}, f32[16,16,512]{2,1,0:T(8,128)}, u32[]{:S(2)}) copy-start(f32[16,16,512]{2,1,0:T(8,128)} %param.10) | copy-start | bytes 1572868
  5.9 1.0 %copy-start.3 = (f32[16,16,512]{2,1,0:T(8,128)S(1)}, f32[16,16,512]{2,1,0:T(8,128)}, u32[]{:S(2)}) copy-start(f32[16,16,512]{2,1,0:T(8,128)} %param.11) | copy-start | bytes 1572868
  7.0 1.0 %copy-start.4 = (s32[16,16,512]{2,1,0:T(8,128)S(1)}, s32[16,16,512]{2,1,0:T(8,128)}, u32[]{:S(2)}) copy-start(s32[16,16,512]{2,1,0:T(8,128)} %param.12) | copy-start | bytes 1572868
  8.0 1.0 %copy-start.5 = (bf16[2,256,512]{2,1,0:T(8,128)(2,1)S(1)}, bf16[2,256,512]{2,1,0:T(8,128)(2,1)}, u32[]{:S(2)}) copy-start(bf16[2,256,512]{2,1,0:T(8,128)(2,1)} %constant.6.clone.star_hbm) | copy-start | bytes 1572868
  9.1 0.7 %copy-start.6 = (f32[256]{0:T(256)S(1)}, f32[256]{0:T(256)}, u32[]{:S(2)}) copy-start(f32[256]{0:T(256)} %wave_ref.1) | copy-start | bytes 3076
  9.7 0.7 %copy-start.7 = (s32[4]{0:T(128)S(1)}, s32[4]{0:T(128)}, u32[]{:S(2)}) copy-start(s32[4]{0:T(128)} %cells_ref.1) | copy-start | bytes 52
  10.4 0.7 %copy-start.8 = (s32[4]{0:T(128)S(1)}, s32[4]{0:T(128)}, u32[]{:S(2)}) copy-start(s32[4]{0:T(128)} %samples_ref.1) | copy-start | bytes 52
  11.1 0.7 %copy-start.9 = (f32[16]{0:T(128)S(1)}, f32[16]{0:T(128)}, u32[]{:S(2)}) copy-start(f32[16]{0:T(128)} %table_ref.1) | copy-start | bytes 196

commit v2 on v1

--- a/solution.py
+++ b/solution.py
@@ -19,6 +19,7 @@
 QUANT_STEP = 0.5
 W = 4
 MESH = pl.DeviceIdType.MESH
+VMEM_BYTES = 62 * 1024 * 1024
 
 
 def lift_matrix(size):
@@ -117,9 +118,10 @@
 
 def kernel(
     rows_x, rows_y,
-    cells_ref, samples_ref, wave_ref, table_ref,
+    cells_hbm, samples_hbm, wave_hbm, table_hbm,
     now_hbm, old_hbm, classes_hbm, star_hbm, along_hbm, lift_hbm,
     next_hbm, mid_hbm, code_hbm,
+    cells_ref, samples_ref, wave_ref, table_ref,
     now, old, classes, star, along, lift,
     courant, mid, later, acc, packed, halo_a, halo_b, halo_c,
     local_sem, out_sem, send_sem, recv_sem,
@@ -143,6 +145,8 @@
                 (now_hbm, now), (classes_hbm, classes), (old_hbm, old),
                 (star_hbm, star), (along_hbm, along),
                 (lift_hbm.at[kind_x * 3 + kind_y], lift),
+                (cells_hbm, cells_ref), (samples_hbm, samples_ref),
+                (wave_hbm, wave_ref), (table_hbm, table_ref),
             ]
         )
     ]
@@ -238,6 +242,8 @@
     each(first_sends[2:], start)
     each(first_sends[:2], start)
 
+    for pull in pulls[6:]:
+        pull.wait()
     wave_len = wave_ref.shape[0]
     all_y = rows_y * count_y
     shots = []
@@ -321,6 +327,15 @@
     code_out.wait()
 
 
+def put_out(*refs):
+    sources, targets, sems = refs[:3], refs[3:6], refs[6]
+    copies = [pltpu.make_async_copy(sources[i], targets[i], sems.at[i]) for i in range(3)]
+    for copy in copies:
+        copy.start()
+    for copy in copies:
+        copy.wait()
+
+
 def shards(pressure_now, pressure_old, classes, class_table, wavelet, source_cells, samples):
     rows_x, rows_y, depth = pressure_now.shape
     size = rows_x * rows_y
@@ -329,16 +344,19 @@
     halo_rows = star.shape[2] - size
     wide_rows = lift.shape[3] - size
     face_y = W * rows_x
-    any_spec = pl.BlockSpec(memory_space=pl.ANY)
-    smem = pl.BlockSpec(memory_space=pltpu.SMEM)
+    hbm = pl.BlockSpec(memory_space=pltpu.HBM)
     f32 = jnp.float32
     out = jax.ShapeDtypeStruct(flat, f32)
     results = pl.pallas_call(
         functools.partial(kernel, rows_x, rows_y),
         out_shape=(out, out, out),
-        in_specs=[smem] * 4 + [any_spec] * 6,
-        out_specs=(any_spec,) * 3,
+        in_specs=[hbm] * 10,
+        out_specs=(hbm,) * 3,
         scratch_shapes=[
+            pltpu.SMEM(source_cells.shape, jnp.int32),
+            pltpu.SMEM(samples.shape, jnp.int32),
+            pltpu.SMEM(wavelet.shape, f32),
+            pltpu.SMEM(class_table.shape, f32),
             pltpu.VMEM(flat, f32),
             pltpu.VMEM(flat, f32),
             pltpu.VMEM(flat, jnp.int32),
@@ -353,19 +371,27 @@
             pltpu.VMEM((halo_rows, depth), f32),
             pltpu.VMEM((halo_rows, depth), f32),
             pltpu.VMEM((wide_rows, depth), f32),
-            pltpu.SemaphoreType.DMA((6,)),
+            pltpu.SemaphoreType.DMA((10,)),
             pltpu.SemaphoreType.DMA((3,)),
             pltpu.SemaphoreType.DMA((16,)),
             pltpu.SemaphoreType.DMA((16,)),
         ],
         compiler_params=pltpu.CompilerParams(
-            collective_id=0, has_side_effects=True, vmem_limit_bytes=40 * 1024 * 1024
+            collective_id=0, has_side_effects=True, vmem_limit_bytes=VMEM_BYTES
         ),
     )(
         source_cells, samples, wavelet, class_table,
         pressure_now.reshape(flat), pressure_old.reshape(flat), classes.reshape(flat),
         jnp.asarray(star), jnp.asarray(along), jnp.asarray(lift),
     )
+    results = pl.pallas_call(
+        put_out,
+        out_shape=(out, out, out),
+        in_specs=[hbm] * 3,
+        out_specs=(hbm,) * 3,
+        scratch_shapes=[pltpu.SemaphoreType.DMA((3,))],
+        compiler_params=pltpu.CompilerParams(vmem_limit_bytes=VMEM_BYTES),
+    )(*results)
     return tuple(result.reshape(pressure_now.shape) for result in results)
 
 

time: 36.8 us -> 71.7 us (1.95)
  Pallas kernels: 22.1 us -> 70.6 us
  local copies, waits for them, and re-layouts: 13.4 us -> 0 us
    pallas_call x0 -> x1, Pallas kernels: none -> 48.8 us  [shards(): pl.pallas_call(put_out, out_shape=(out, out, out), in_specs=[hbm] * 3, ou...]
    unnamed x23 -> x0, local copies, waits for them, and re-layouts: 13.4 us -> none
where the time goes in v2:
time: 71.7 us; the launch traced here: 71.2 us
  Pallas kernels  70.6 us (98%)
    pallas_call x1, Pallas kernels, shards(): pl.pallas_call(put_out, out_shape=(out, out, out), in_specs=[hbm] * 3, ou...  48.8 us
    pallas_call x1, Pallas kernels, shards(): pl.pallas_call(functools.partial(kernel, rows_x, rows_y), out_shape=(out,...  21.8 us

profile of v2, /device:TPU:1, one launch (start us, length us, event | category | flops | bytes accessed | tf_op | source)
XLA Modules:
  0.0 71.2 jit_solution(6843561508960746199)
XLA Ops:
  0.6 21.8 %shard_map.121 = (f32[256,512]{1,0:T(8,128)}, f32[256,512]{1,0:T(8,128)}, f32[256,512]{1,0:T(8,128)}) custom-call(s32[4]{0:T(128)} %cells_hbm.1, s32[4]{0:T(128)} %samples_hbm.1, f32[256]{0:T(256)} %wave_hbm.1, f32[16]{0:T(128)} %table_hbm.1, f32[256,512]{1,0:T(8,128)} %bitcast.6, f32[256,512]{1,0:T(8,128)} %bitcast.7, s32[256,512]{1,0:T(8,128)} %bitcast.8, ...), custom_call_target="tpu_custom_call" | custom-call | tf_op jit(solution)/shard_map/pallas_call | solution.py:350
  22.5 48.8 %shard_map.122 = (f32[256,512]{1,0:T(8,128)}, f32[256,512]{1,0:T(8,128)}, f32[256,512]{1,0:T(8,128)}) custom-call(f32[256,512]{1,0:T(8,128)} %get-tuple-element.9.refs_0_, f32[256,512]{1,0:T(8,128)} %get-tuple-element.10.refs_1_, f32[256,512]{1,0:T(8,128)} %get-tuple-element.11.refs_2_), custom_call_target="tpu_custom_call" | custom-call | tf_op jit(solution)/shard_map/pallas_call | solution.py:387

commit v3 on v2

--- a/solution.py
+++ b/solution.py
@@ -19,7 +19,7 @@
 QUANT_STEP = 0.5
 W = 4
 MESH = pl.DeviceIdType.MESH
-VMEM_BYTES = 62 * 1024 * 1024
+VMEM_BYTES = 32 * 1024 * 1024
 
 
 def lift_matrix(size):
@@ -344,6 +344,7 @@
     halo_rows = star.shape[2] - size
     wide_rows = lift.shape[3] - size
     face_y = W * rows_x
+    any_spec = pl.BlockSpec(memory_space=pl.ANY)
     hbm = pl.BlockSpec(memory_space=pltpu.HBM)
     f32 = jnp.float32
     out = jax.ShapeDtypeStruct(flat, f32)
@@ -351,7 +352,7 @@
         functools.partial(kernel, rows_x, rows_y),
         out_shape=(out, out, out),
         in_specs=[hbm] * 10,
-        out_specs=(hbm,) * 3,
+        out_specs=(any_spec,) * 3,
         scratch_shapes=[
             pltpu.SMEM(source_cells.shape, jnp.int32),
             pltpu.SMEM(samples.shape, jnp.int32),
@@ -379,15 +380,18 @@
         compiler_params=pltpu.CompilerParams(
             collective_id=0, has_side_effects=True, vmem_limit_bytes=VMEM_BYTES
         ),
-    )(
-        source_cells, samples, wavelet, class_table,
-        pressure_now.reshape(flat), pressure_old.reshape(flat), classes.reshape(flat),
-        jnp.asarray(star), jnp.asarray(along), jnp.asarray(lift),
-    )
+    )(*[
+        pltpu.with_memory_space_constraint(operand, pltpu.HBM)
+        for operand in (
+            source_cells, samples, wavelet, class_table,
+            pressure_now.reshape(flat), pressure_old.reshape(flat), classes.reshape(flat),
+            jnp.asarray(star), jnp.asarray(along), jnp.asarray(lift),
+        )
+    ])
     results = pl.pallas_call(
         put_out,
         out_shape=(out, out, out),
-        in_specs=[hbm] * 3,
+        in_specs=[any_spec] * 3,
         out_specs=(hbm,) * 3,
         scratch_shapes=[pltpu.SemaphoreType.DMA((3,))],
         compiler_params=pltpu.CompilerParams(vmem_limit_bytes=VMEM_BYTES),

time: 71.7 us -> 23.3 us (0.32)
  Pallas kernels: 70.6 us -> 22.3 us
    pallas_call x1, Pallas kernels: 48.8 us -> 1.17 us  [shards(): pl.pallas_call(put_out, out_shape=(out, out, out), in_specs=[any_spec] *...]
where the time goes in v3:
time: 23.3 us; the launch traced here: 22.9 us
  Pallas kernels  22.3 us (96%)
  between operations  0.64 us (3%)
    pallas_call x1, Pallas kernels, shards(): pl.pallas_call(functools.partial(kernel, rows_x, rows_y), out_shape=(out,...  21.1 us
    pallas_call x1, Pallas kernels, shards(): pl.pallas_call(put_out, out_shape=(out, out, out), in_specs=[any_spec] *...  1.17 us

profile of v3, /device:TPU:1, one launch (start us, length us, event | category | flops | bytes accessed | tf_op | source)
XLA Modules:
  0.0 22.9 jit_solution(10257038387350053765)
XLA Ops:
  0.6 21.1 %shard_map.121 = (f32[256,512]{1,0:T(8,128)S(1)}, f32[256,512]{1,0:T(8,128)S(1)}, f32[256,512]{1,0:T(8,128)S(1)}) custom-call(s32[4]{0:T(128)} %cells_hbm.1, s32[4]{0:T(128)} %samples_hbm.1, f32[256]{0:T(256)} %wave_hbm.1, f32[16]{0:T(128)} %table_hbm.1, f32[256,512]{1,0:T(8,128)} %bitcast.6, f32[256,512]{1,0:T(8,128)} %bitcast.7, s32[256,512]{1,0:T(8,128)} %bitcast.8, ...), custom_call_target="tpu_custom_call" | custom-call | tf_op jit(solution)/shard_map/pallas_call | solution.py:351
  21.7 1.2 %shard_map.122 = (f32[256,512]{1,0:T(8,128)}, f32[256,512]{1,0:T(8,128)}, f32[256,512]{1,0:T(8,128)}) custom-call(f32[256,512]{1,0:T(8,128)S(1)} %get-tuple-element.9.refs_0_, f32[256,512]{1,0:T(8,128)S(1)} %get-tuple-element.10.refs_1_, f32[256,512]{1,0:T(8,128)S(1)} %get-tuple-element.11.refs_2_), custom_call_target="tpu_custom_call" | custom-call | tf_op jit(solution)/shard_map/pallas_call | solution.py:391

commit v4 on v3

--- a/solution.py
+++ b/solution.py
@@ -19,6 +19,7 @@
 QUANT_STEP = 0.5
 W = 4
 MESH = pl.DeviceIdType.MESH
+PARTS = 2
 VMEM_BYTES = 32 * 1024 * 1024
 
 
@@ -130,6 +131,7 @@
     size = rows_x * rows_y
     face_x, face_y, corner = W * rows_y, W * rows_x, W * W
     faces = 2 * face_x + 2 * face_y
+    width = depth // PARTS
     at_x, at_y = lax.axis_index("gx"), lax.axis_index("gy")
     count_x, count_y = lax.axis_size("gx"), lax.axis_size("gy")
     shot = lax.axis_index("shot")
@@ -168,30 +170,32 @@
         def _(dx=dx, dy=dy):
             pl.semaphore_signal(barrier, inc=1, device_id=device(dx, dy), device_id_type=MESH)
 
-    def pack(source, where):
+    def pack(source, where, part):
+        lanes = slice(part * width, (part + 1) * width)
         for x in range(0, rows_x, 2):
             first, second = x * rows_y, (x + 1) * rows_y
-            packed[where, 0, x * W : (x + 2) * W, :] = jnp.concatenate(
-                [source[first : first + W, :], source[second : second + W, :]], axis=0
+            packed[where, 0, x * W : (x + 2) * W, lanes] = jnp.concatenate(
+                [source[first : first + W, lanes], source[second : second + W, lanes]], axis=0
             )
-            packed[where, 1, x * W : (x + 2) * W, :] = jnp.concatenate(
-                [source[first + rows_y - W : second, :],
-                 source[second + rows_y - W : second + rows_y, :]], axis=0
+            packed[where, 1, x * W : (x + 2) * W, lanes] = jnp.concatenate(
+                [source[first + rows_y - W : second, lanes],
+                 source[second + rows_y - W : second + rows_y, lanes]], axis=0
             )
 
     slots = [(0, face_x), (face_x, face_x), (2 * face_x, face_y), (2 * face_x + face_y, face_y)]
     slots += [(faces + i * corner, corner) for i in range(4)]
 
-    def exchange(source, halo, where, base, with_corners):
+    def exchange(source, halo, where, base, part, with_corners):
+        lanes = pl.ds(part * width, width)
         ends = [
-            source.at[pl.ds(0, face_x)],
-            source.at[pl.ds(size - face_x, face_x)],
-            packed.at[where, 0],
-            packed.at[where, 1],
-            packed.at[where, 0, pl.ds(0, corner)],
-            packed.at[where, 1, pl.ds(0, corner)],
-            packed.at[where, 0, pl.ds(face_y - corner, corner)],
-            packed.at[where, 1, pl.ds(face_y - corner, corner)],
+            source.at[pl.ds(0, face_x), lanes],
+            source.at[pl.ds(size - face_x, face_x), lanes],
+            packed.at[where, 0, pl.ds(0, face_y), lanes],
+            packed.at[where, 1, pl.ds(0, face_y), lanes],
+            packed.at[where, 0, pl.ds(0, corner), lanes],
+            packed.at[where, 1, pl.ds(0, corner), lanes],
+            packed.at[where, 0, pl.ds(face_y - corner, corner), lanes],
+            packed.at[where, 1, pl.ds(face_y - corner, corner), lanes],
         ]
         opposite = [1, 0, 3, 2, 7, 6, 5, 4]
         sends, arrivals = [], []
@@ -201,13 +205,13 @@
                 start, length = slots[to]
                 found.append((has, pltpu.make_async_remote_copy(
                     src_ref=ends[i],
-                    dst_ref=halo.at[pl.ds(start, length)],
-                    send_sem=send_sem.at[base + i],
-                    recv_sem=recv_sem.at[base + to],
+                    dst_ref=halo.at[pl.ds(start, length), lanes],
+                    send_sem=send_sem.at[part, base + i],
+                    recv_sem=recv_sem.at[part, base + to],
                     device_id=device(dx, dy),
                     device_id_type=MESH,
                 )))
-        return sends, arrivals
+        return sends[2:] + sends[:2], arrivals
 
     def each(copies, act):
         for has, copy in copies:
@@ -219,11 +223,12 @@
     landed = lambda copy: copy.wait_recv()
     sent = lambda copy: copy.wait_send()
 
-    first_sends, first_lands = exchange(now, halo_a, 0, 0, False)
-    second_sends, second_lands = exchange(mid, halo_b, 1, 4, False)
-    third_sends, third_lands = exchange(later, halo_c, 2, 8, True)
-
-    for halo, lands in ((halo_a, first_lands), (halo_b, second_lands), (halo_c, third_lands)):
+    parts = range(PARTS)
+    first = [exchange(now, halo_a, 0, 0, part, False) for part in parts]
+    second = [exchange(mid, halo_b, 1, 4, part, False) for part in parts]
+    third = [exchange(later, halo_c, 2, 8, part, True) for part in parts]
+
+    for halo, lands in ((halo_a, first[0][1]), (halo_b, second[0][1]), (halo_c, third[0][1])):
         for i, (has, _) in enumerate(lands):
             begin, length = slots[i]
 
@@ -235,12 +240,13 @@
         halo_c[tail:, :] = jnp.zeros((halo_c.shape[0] - tail, depth), jnp.float32)
 
     pulls[0].wait()
-    pack(now, 0)
+    for part in parts:
+        pack(now, 0, part)
     near_x = low_x.astype(jnp.int32) + high_x.astype(jnp.int32)
     near_y = low_y.astype(jnp.int32) + high_y.astype(jnp.int32)
     pl.semaphore_wait(barrier, near_x + near_y + near_x * near_y)
-    each(first_sends[2:], start)
-    each(first_sends[:2], start)
+    for part in parts:
+        each(first[part][0], start)
 
     for pull in pulls[6:]:
         pull.wait()
@@ -288,40 +294,46 @@
         own = [star[0, :, :size], star[1, :, :size]]
         acc[...] = product(own, both) + product(both, (along[0], along[1]))
 
-    def outer(halo):
-        return product([star[0, :, size:], star[1, :, size:]], split(halo[...]))
-
+    def outer(halo, lanes):
+        return product([star[0, :, size:], star[1, :, size:]], split(halo[:, lanes]))
+
+    cuts = [slice(part * width, (part + 1) * width) for part in parts]
     inner(now)
-    each(first_lands, landed)
-    mid[...] = old[...] + courant[...] * (acc[...] + outer(halo_a))
-    each(second_sends[:2], start)
-    pack(mid, 1)
-    each(second_sends[2:], start)
+    for part, lanes in enumerate(cuts):
+        each(first[part][1], landed)
+        mid[:, lanes] = old[:, lanes] + courant[:, lanes] * (acc[:, lanes] + outer(halo_a, lanes))
+        pack(mid, 1, part)
+        each(second[part][0], start)
     mid_out = pltpu.make_async_copy(mid, mid_hbm, out_sem.at[0])
     mid_out.start()
 
     later[...] = later[...] + 2.0 * mid[...]
     inner(mid)
-    each(second_lands, landed)
-    later[...] = later[...] + courant[...] * (acc[...] + outer(halo_b))
-    each(third_sends[:2], start)
-    pack(later, 2)
-    each(third_sends[2:], start)
+    for part, lanes in enumerate(cuts):
+        each(second[part][1], landed)
+        later[:, lanes] = later[:, lanes] + courant[:, lanes] * (
+            acc[:, lanes] + outer(halo_b, lanes)
+        )
+        pack(later, 2, part)
+        each(third[part][0], start)
     next_out = pltpu.make_async_copy(later, next_hbm, out_sem.at[1])
     next_out.start()
 
     pulls[5].wait()
     acc[...] = product([lift[0, :, :size], lift[1, :, :size]], split(later[...]))
-    each(third_lands, landed)
-    lifted = acc[...] + product([lift[0, :, size:], lift[1, :, size:]], split(halo_c[...]))
-    lifted = product(split(lifted), (along[2], along[3]))
+    lifted = None
+    for part, lanes in enumerate(cuts):
+        each(third[part][1], landed)
+        beside = [lift[0, :, size:], lift[1, :, size:]]
+        flat = acc[:, lanes] + product(beside, split(halo_c[:, lanes]))
+        term = product(split(flat), (along[2, lanes, :], along[3, lanes, :]))
+        lifted = term if lifted is None else lifted + term
     shrunk = jnp.maximum(jnp.abs(lifted) - DEAD_ZONE, 0.0) / QUANT_STEP
     acc[...] = jnp.where(lifted < 0.0, -shrunk, shrunk)
     code_out = pltpu.make_async_copy(acc, code_hbm, out_sem.at[2])
     code_out.start()
-    each(first_sends, sent)
-    each(second_sends, sent)
-    each(third_sends, sent)
+    for sends, _ in first + second + third:
+        each(sends, sent)
     mid_out.wait()
     next_out.wait()
     code_out.wait()
@@ -374,8 +386,8 @@
             pltpu.VMEM((wide_rows, depth), f32),
             pltpu.SemaphoreType.DMA((10,)),
             pltpu.SemaphoreType.DMA((3,)),
-            pltpu.SemaphoreType.DMA((16,)),
-            pltpu.SemaphoreType.DMA((16,)),
+            pltpu.SemaphoreType.DMA((PARTS, 16)),
+            pltpu.SemaphoreType.DMA((PARTS, 16)),
         ],
         compiler_params=pltpu.CompilerParams(
             collective_id=0, has_side_effects=True, vmem_limit_bytes=VMEM_BYTES

time: 23.3 us -> 22 us (0.944)
  the two profiles are of different devices: /device:TPU:1 before, /device:TPU:0 now
where the time goes in v4:
time: 22 us; the launch traced here: 21.8 us
  Pallas kernels  21.2 us (96%)
  between operations  0.64 us (3%)
    pallas_call x1, Pallas kernels, shards(): pl.pallas_call(functools.partial(kernel, rows_x, rows_y), out_shape=(out,...  20 us
    pallas_call x1, Pallas kernels, shards(): pl.pallas_call(put_out, out_shape=(out, out, out), in_specs=[any_spec] *...  1.17 us

profile of v4, /device:TPU:0, one launch (start us, length us, event | category | flops | bytes accessed | tf_op | source)
XLA Modules:
  0.0 21.8 jit_solution(9679166466067817885)
XLA Ops:
  0.6 20.0 %shard_map.121 = (f32[256,512]{1,0:T(8,128)S(1)}, f32[256,512]{1,0:T(8,128)S(1)}, f32[256,512]{1,0:T(8,128)S(1)}) custom-call(s32[4]{0:T(128)} %cells_hbm.1, s32[4]{0:T(128)} %samples_hbm.1, f32[256]{0:T(256)} %wave_hbm.1, f32[16]{0:T(128)} %table_hbm.1, f32[256,512]{1,0:T(8,128)} %bitcast.6, f32[256,512]{1,0:T(8,128)} %bitcast.7, s32[256,512]{1,0:T(8,128)} %bitcast.8, ...), custom_call_target="tpu_custom_call" | custom-call | tf_op jit(solution)/shard_map/pallas_call | solution.py:363
  20.7 1.2 %shard_map.122 = (f32[256,512]{1,0:T(8,128)}, f32[256,512]{1,0:T(8,128)}, f32[256,512]{1,0:T(8,128)}) custom-call(f32[256,512]{1,0:T(8,128)S(1)} %get-tuple-element.9.refs_0_, f32[256,512]{1,0:T(8,128)S(1)} %get-tuple-element.10.refs_1_, f32[256,512]{1,0:T(8,128)S(1)} %get-tuple-element.11.refs_2_), custom_call_target="tpu_custom_call" | custom-call | tf_op jit(solution)/shard_map/pallas_call | solution.py:403

commit v5 on v4

--- a/solution.py
+++ b/solution.py
@@ -56,22 +56,49 @@
     return np.stack([high, low], axis=-3)
 
 
-def halo_cells(rows_x, rows_y):
+def edge_sums(size):
+    low, high = np.zeros((2, size)), np.zeros((2, size))
+    low[0, 0] = low[1, 1] = high[0, size - 1] = high[1, size - 2] = 1.0
+    low[1, 2] = high[0, size - 2] = LIFT_ALPHA
+    high[1, size - 3] = LIFT_BETA
+    high[1, size - 4] = LIFT_BETA * LIFT_ALPHA
+    high[1, size - 2] += LIFT_BETA * LIFT_ALPHA
+    return low, high
+
+
+def lift_by_sums(size, first, last):
+    whole = lift_matrix(size)
+    low, high = edge_sums(size)
+    below = whole[:, :W] @ np.linalg.pinv(high[:, size - W :])
+    above = whole[:, W + size :] @ np.linalg.pinv(low[:, :W])
+    assert np.allclose(below @ high[:, size - W :], whole[:, :W], atol=1e-12)
+    assert np.allclose(above @ low[:, :W], whole[:, W + size :], atol=1e-12)
+    own = reflected(whole, first, last)[:, W : W + size]
+    return own, below * (not first), above * (not last)
+
+
+def sum_rows(own_x, sides_x, own_y, sides_y):
+    rows = [np.einsum("ix,jy->ijxy", side, own_y) for side in sides_x]
+    rows += [np.einsum("ix,jy->ijxy", own_x, side) for side in sides_y]
+    for side_x in sides_x:
+        for side_y in sides_y:
+            corner = np.einsum("ix,jy->ijxy", side_x, side_y)
+            rows.append(np.concatenate([corner, np.zeros_like(corner)]))
+    return np.concatenate([row.reshape(-1, row.shape[2] * row.shape[3]) for row in rows])
+
+
+def face_cells(rows_x, rows_y):
     low, x_high, y_high = range(-W, 0), range(rows_x, rows_x + W), range(rows_y, rows_y + W)
     cells = [(x, y) for x in low for y in range(rows_y)]
     cells += [(x, y) for x in x_high for y in range(rows_y)]
     cells += [(x, y) for x in range(rows_x) for y in low]
     cells += [(x, y) for x in range(rows_x) for y in y_high]
-    faces = len(cells)
-    for side_x in (low, x_high):
-        for side_y in (low, y_high):
-            cells += [(x, y) for x in side_x for y in side_y]
-    return cells, faces
+    return cells
 
 
 @functools.lru_cache(None)
 def tables(rows_x, rows_y, depth):
-    cells, faces = halo_cells(rows_x, rows_y)
+    cells = face_cells(rows_x, rows_y)
     own = [(x, y) for x in range(rows_x) for y in range(rows_y)]
     everywhere = np.array(own + cells)
     target = np.array(own)
@@ -80,7 +107,6 @@
     weights = np.array(list(STENCIL_WEIGHTS) + [0.0])
     star = np.where(gap_y == 0, weights[np.minimum(gap_x, W + 1)], 0.0)
     star = star + np.where(gap_x == 0, weights[np.minimum(gap_y, W + 1)], 0.0)
-    star = star[:, : len(own) + faces]
     spot = np.arange(depth)
     along = weights[np.minimum(np.abs(spot[:, None] - spot[None, :]), W + 1)]
     depth_lift = reflected(lift_matrix(depth), True, True)[:, W : W + depth].T
@@ -88,14 +114,16 @@
     lifts = []
     for kind_x in kinds:
         for kind_y in kinds:
-            by_x = reflected(lift_matrix(rows_x), *kind_x)[:, everywhere[:, 0] + W]
-            by_y = reflected(lift_matrix(rows_y), *kind_y)[:, everywhere[:, 1] + W]
-            lifts.append(by_x[target[:, 0]] * by_y[target[:, 1]])
+            own_x, below_x, above_x = lift_by_sums(rows_x, *kind_x)
+            own_y, below_y, above_y = lift_by_sums(rows_y, *kind_y)
+            beside = sum_rows(own_x.T, (below_x.T, above_x.T), own_y.T, (below_y.T, above_y.T))
+            lifts.append(np.concatenate([np.kron(own_x, own_y), beside.T], axis=1))
     lifts = np.stack(lifts)
     spare = -lifts.shape[2] % 128
     lifts = np.pad(lifts, ((0, 0), (0, 0), (0, spare)))
+    sums = sum_rows(np.eye(rows_x), edge_sums(rows_x), np.eye(rows_y), edge_sums(rows_y))
     depth_both = np.concatenate([halves(along), halves(depth_lift)])
-    return halves(star), depth_both, halves(lifts)
+    return halves(star), depth_both, halves(lifts), halves(sums)
 
 
 def split(values):
@@ -120,17 +148,18 @@
 def kernel(
     rows_x, rows_y,
     cells_hbm, samples_hbm, wave_hbm, table_hbm,
-    now_hbm, old_hbm, classes_hbm, star_hbm, along_hbm, lift_hbm,
+    now_hbm, old_hbm, classes_hbm, star_hbm, along_hbm, lift_hbm, sums_hbm,
     next_hbm, mid_hbm, code_hbm,
     cells_ref, samples_ref, wave_ref, table_ref,
-    now, old, classes, star, along, lift,
-    courant, mid, later, acc, packed, halo_a, halo_b, halo_c,
+    now, old, classes, star, along, lift, sums,
+    courant, mid, later, acc, packed, bundle, halo_a, halo_b, halo_c,
     local_sem, out_sem, send_sem, recv_sem,
 ):
     depth = now.shape[1]
     size = rows_x * rows_y
-    face_x, face_y, corner = W * rows_y, W * rows_x, W * W
-    faces = 2 * face_x + 2 * face_y
+    face_x, face_y = W * rows_y, W * rows_x
+    slim_x, slim_y, corner = 2 * rows_y, 2 * rows_x, 8
+    slim = 2 * slim_x + 2 * slim_y
     width = depth // PARTS
     at_x, at_y = lax.axis_index("gx"), lax.axis_index("gy")
     count_x, count_y = lax.axis_size("gx"), lax.axis_size("gy")
@@ -146,7 +175,7 @@
             [
                 (now_hbm, now), (classes_hbm, classes), (old_hbm, old),
                 (star_hbm, star), (along_hbm, along),
-                (lift_hbm.at[kind_x * 3 + kind_y], lift),
+                (lift_hbm.at[kind_x * 3 + kind_y], lift), (sums_hbm, sums),
                 (cells_hbm, cells_ref), (samples_hbm, samples_ref),
                 (wave_hbm, wave_ref), (table_hbm, table_ref),
             ]
@@ -183,26 +212,29 @@
             )
 
     slots = [(0, face_x), (face_x, face_x), (2 * face_x, face_y), (2 * face_x + face_y, face_y)]
-    slots += [(faces + i * corner, corner) for i in range(4)]
-
-    def exchange(source, halo, where, base, part, with_corners):
-        lanes = pl.ds(part * width, width)
-        ends = [
+    thin = [(0, slim_x), (slim_x, slim_x), (2 * slim_x, slim_y), (2 * slim_x + slim_y, slim_y)]
+    thin += [(slim + i * corner, corner) for i in range(4)]
+
+    def layers(source, where, lanes):
+        return [
             source.at[pl.ds(0, face_x), lanes],
             source.at[pl.ds(size - face_x, face_x), lanes],
             packed.at[where, 0, pl.ds(0, face_y), lanes],
             packed.at[where, 1, pl.ds(0, face_y), lanes],
-            packed.at[where, 0, pl.ds(0, corner), lanes],
-            packed.at[where, 1, pl.ds(0, corner), lanes],
-            packed.at[where, 0, pl.ds(face_y - corner, corner), lanes],
-            packed.at[where, 1, pl.ds(face_y - corner, corner), lanes],
         ]
+
+    def combined(lanes):
+        return [bundle.at[pl.ds(begin, length), lanes] for begin, length in thin]
+
+    def exchange(ends, halo, places, base, part):
+        lanes = pl.ds(part * width, width)
+        ends = ends(lanes)
         opposite = [1, 0, 3, 2, 7, 6, 5, 4]
         sends, arrivals = [], []
-        for i in range(8 if with_corners else 4):
+        for i in range(len(ends)):
             dx, dy, has = partners[i]
             for to, found in ((opposite[i], sends), (i, arrivals)):
-                start, length = slots[to]
+                start, length = places[to]
                 found.append((has, pltpu.make_async_remote_copy(
                     src_ref=ends[i],
                     dst_ref=halo.at[pl.ds(start, length), lanes],
@@ -224,18 +256,21 @@
     sent = lambda copy: copy.wait_send()
 
     parts = range(PARTS)
-    first = [exchange(now, halo_a, 0, 0, part, False) for part in parts]
-    second = [exchange(mid, halo_b, 1, 4, part, False) for part in parts]
-    third = [exchange(later, halo_c, 2, 8, part, True) for part in parts]
-
-    for halo, lands in ((halo_a, first[0][1]), (halo_b, second[0][1]), (halo_c, third[0][1])):
+    cuts = [slice(part * width, (part + 1) * width) for part in parts]
+    first = [exchange(functools.partial(layers, now, 0), halo_a, slots, 0, p) for p in parts]
+    second = [exchange(functools.partial(layers, mid, 1), halo_b, slots, 4, p) for p in parts]
+    third = [exchange(combined, halo_c, thin, 8, p) for p in parts]
+
+    for halo, places, lands in (
+        (halo_a, slots, first[0][1]), (halo_b, slots, second[0][1]), (halo_c, thin, third[0][1])
+    ):
         for i, (has, _) in enumerate(lands):
-            begin, length = slots[i]
+            begin, length = places[i]
 
             @pl.when(jnp.logical_not(has))
             def _(halo=halo, begin=begin, length=length):
                 halo[begin : begin + length, :] = jnp.zeros((length, depth), jnp.float32)
-    tail = faces + 4 * corner
+    tail = slim + 4 * corner
     if halo_c.shape[0] > tail:
         halo_c[tail:, :] = jnp.zeros((halo_c.shape[0] - tail, depth), jnp.float32)
 
@@ -248,7 +283,7 @@
     for part in parts:
         each(first[part][0], start)
 
-    for pull in pulls[6:]:
+    for pull in pulls[7:]:
         pull.wait()
     wave_len = wave_ref.shape[0]
     all_y = rows_y * count_y
@@ -289,15 +324,31 @@
     pulls[3].wait()
     pulls[4].wait()
 
+    def deep(both, at, lanes):
+        return product([b[:, lanes] for b in both], [along[at, lanes, lanes], along[at + 1, lanes, lanes]])
+
+    def crossing(both, at, source, target):
+        return product(
+            [b[:, source] for b in both], [along[at, source, target], along[at + 1, source, target]]
+        )
+
+    seams = [
+        (slice(part * width - 128, part * width), slice(part * width, part * width + 128))
+        for part in range(1, PARTS)
+    ]
+
     def inner(field):
         both = split(field[...])
-        own = [star[0, :, :size], star[1, :, :size]]
-        acc[...] = product(own, both) + product(both, (along[0], along[1]))
+        for lanes in cuts:
+            own = product([star[0, :, :size], star[1, :, :size]], [b[:, lanes] for b in both])
+            acc[:, lanes] = own + deep(both, 0, lanes)
+        for left, right in seams:
+            acc[:, left] += crossing(both, 0, right, left)
+            acc[:, right] += crossing(both, 0, left, right)
 
     def outer(halo, lanes):
         return product([star[0, :, size:], star[1, :, size:]], split(halo[:, lanes]))
 
-    cuts = [slice(part * width, (part + 1) * width) for part in parts]
     inner(now)
     for part, lanes in enumerate(cuts):
         each(first[part][1], landed)
@@ -309,25 +360,37 @@
 
     later[...] = later[...] + 2.0 * mid[...]
     inner(mid)
+    pulls[5].wait()
+    pulls[6].wait()
+    lifted_own = []
     for part, lanes in enumerate(cuts):
         each(second[part][1], landed)
         later[:, lanes] = later[:, lanes] + courant[:, lanes] * (
             acc[:, lanes] + outer(halo_b, lanes)
         )
-        pack(later, 2, part)
+        both = split(later[:, lanes])
+        bundle[:, lanes] = product((sums[0], sums[1]), both)
         each(third[part][0], start)
+        lifted_own.append(both)
     next_out = pltpu.make_async_copy(later, next_hbm, out_sem.at[1])
     next_out.start()
 
-    pulls[5].wait()
-    acc[...] = product([lift[0, :, :size], lift[1, :, :size]], split(later[...]))
-    lifted = None
+    for lanes, both in zip(cuts, lifted_own):
+        acc[:, lanes] = product([lift[0, :, :size], lift[1, :, :size]], both)
+    pieces = []
     for part, lanes in enumerate(cuts):
         each(third[part][1], landed)
         beside = [lift[0, :, size:], lift[1, :, size:]]
-        flat = acc[:, lanes] + product(beside, split(halo_c[:, lanes]))
-        term = product(split(flat), (along[2, lanes, :], along[3, lanes, :]))
-        lifted = term if lifted is None else lifted + term
+        piece = split(acc[:, lanes] + product(beside, split(halo_c[:, lanes])))
+        pieces.append(piece)
+        courant[:, lanes] = product(piece, (along[2, lanes, lanes], along[3, lanes, lanes]))
+        if part:
+            left, right = seams[part - 1]
+            over = (along[2, left, right], along[3, left, right])
+            courant[:, right] += product([half[:, -128:] for half in pieces[part - 1]], over)
+            back = (along[2, right, left], along[3, right, left])
+            courant[:, left] += product([half[:, :128] for half in piece], back)
+    lifted = courant[...]
     shrunk = jnp.maximum(jnp.abs(lifted) - DEAD_ZONE, 0.0) / QUANT_STEP
     acc[...] = jnp.where(lifted < 0.0, -shrunk, shrunk)
     code_out = pltpu.make_async_copy(acc, code_hbm, out_sem.at[2])
@@ -352,7 +415,7 @@
     rows_x, rows_y, depth = pressure_now.shape
     size = rows_x * rows_y
     flat = (size, depth)
-    star, along, lift = tables(rows_x, rows_y, depth)
+    star, along, lift, sums = tables(rows_x, rows_y, depth)
     halo_rows = star.shape[2] - size
     wide_rows = lift.shape[3] - size
     face_y = W * rows_x
@@ -363,7 +426,7 @@
     results = pl.pallas_call(
         functools.partial(kernel, rows_x, rows_y),
         out_shape=(out, out, out),
-        in_specs=[hbm] * 10,
+        in_specs=[hbm] * 11,
         out_specs=(any_spec,) * 3,
         scratch_shapes=[
             pltpu.SMEM(source_cells.shape, jnp.int32),
@@ -376,15 +439,17 @@
             pltpu.VMEM(star.shape, jnp.bfloat16),
             pltpu.VMEM(along.shape, jnp.bfloat16),
             pltpu.VMEM(lift.shape[1:], jnp.bfloat16),
-            pltpu.VMEM(flat, f32),
-            pltpu.VMEM(flat, f32),
-            pltpu.VMEM(flat, f32),
-            pltpu.VMEM(flat, f32),
-            pltpu.VMEM((3, 2, face_y, depth), f32),
+            pltpu.VMEM(sums.shape, jnp.bfloat16),
+            pltpu.VMEM(flat, f32),
+            pltpu.VMEM(flat, f32),
+            pltpu.VMEM(flat, f32),
+            pltpu.VMEM(flat, f32),
+            pltpu.VMEM((2, 2, face_y, depth), f32),
+            pltpu.VMEM((sums.shape[1], depth), f32),
             pltpu.VMEM((halo_rows, depth), f32),
             pltpu.VMEM((halo_rows, depth), f32),
             pltpu.VMEM((wide_rows, depth), f32),
-            pltpu.SemaphoreType.DMA((10,)),
+            pltpu.SemaphoreType.DMA((11,)),
             pltpu.SemaphoreType.DMA((3,)),
             pltpu.SemaphoreType.DMA((PARTS, 16)),
             pltpu.SemaphoreType.DMA((PARTS, 16)),
@@ -398,6 +463,7 @@
             source_cells, samples, wavelet, class_table,
             pressure_now.reshape(flat), pressure_old.reshape(flat), classes.reshape(flat),
             jnp.asarray(star), jnp.asarray(along), jnp.asarray(lift),
+            jnp.asarray(sums),
         )
     ])
     results = pl.pallas_call(

time: 22 us -> 20.4 us (0.927)
  the two profiles are of different devices: /device:TPU:0 before, /device:TPU:1 now
where the time goes in v5:
time: 20.4 us; the launch traced here: 20.3 us
  Pallas kernels  19.7 us (97%)
  between operations  0.64 us (3%)
    pallas_call x1, Pallas kernels, shards(): pl.pallas_call(functools.partial(kernel, rows_x, rows_y), out_shape=(out,...  18.5 us
    pallas_call x1, Pallas kernels, shards(): pl.pallas_call(put_out, out_shape=(out, out, out), in_specs=[any_spec] *...  1.17 us

profile of v5, /device:TPU:1, one launch (start us, length us, event | category | flops | bytes accessed | tf_op | source)
XLA Modules:
  0.0 20.3 jit_solution(12843564476464369182)
XLA Ops:
  0.6 18.5 %shard_map.130 = (f32[256,512]{1,0:T(8,128)S(1)}, f32[256,512]{1,0:T(8,128)S(1)}, f32[256,512]{1,0:T(8,128)S(1)}) custom-call(s32[4]{0:T(128)} %cells_hbm.1, s32[4]{0:T(128)} %samples_hbm.1, f32[256]{0:T(256)} %wave_hbm.1, f32[16]{0:T(128)} %table_hbm.1, f32[256,512]{1,0:T(8,128)} %bitcast.6, f32[256,512]{1,0:T(8,128)} %bitcast.7, s32[256,512]{1,0:T(8,128)} %bitcast.8, ...), custom_call_target="tpu_custom_call" | custom-call | tf_op jit(solution)/shard_map/pallas_call | solution.py:426
  19.1 1.2 %shard_map.131 = (f32[256,512]{1,0:T(8,128)}, f32[256,512]{1,0:T(8,128)}, f32[256,512]{1,0:T(8,128)}) custom-call(f32[256,512]{1,0:T(8,128)S(1)} %get-tuple-element.9.refs_0_, f32[256,512]{1,0:T(8,128)S(1)} %get-tuple-element.10.refs_1_, f32[256,512]{1,0:T(8,128)S(1)} %get-tuple-element.11.refs_2_), custom_call_target="tpu_custom_call" | custom-call | tf_op jit(solution)/shard_map/pallas_call | solution.py:469

commit v6 on v5

--- a/solution.py
+++ b/solution.py
@@ -181,7 +181,8 @@
             ]
         )
     ]
-    for pull in pulls:
+    pulls[0].start()
+    for pull in pulls[7:]:
         pull.start()
 
     steps = ((-1, low_x, low_y), (1, high_x, high_y))
@@ -275,6 +276,8 @@
         halo_c[tail:, :] = jnp.zeros((halo_c.shape[0] - tail, depth), jnp.float32)
 
     pulls[0].wait()
+    for pull in pulls[1:5]:
+        pull.start()
     for part in parts:
         pack(now, 0, part)
     near_x = low_x.astype(jnp.int32) + high_x.astype(jnp.int32)
@@ -282,6 +285,8 @@
     pl.semaphore_wait(barrier, near_x + near_y + near_x * near_y)
     for part in parts:
         each(first[part][0], start)
+    for pull in pulls[5:7]:
+        pull.start()
 
     for pull in pulls[7:]:
         pull.wait()
@@ -302,25 +307,29 @@
     pulls[1].wait()
     pulls[2].wait()
 
-    def plane(x, carry):
+    place = lax.broadcasted_iota(jnp.int32, (rows_y, depth), 0) * depth
+    place = place + lax.broadcasted_iota(jnp.int32, (rows_y, depth), 1)
+
+    def with_sources(base, x, step):
+        for shot_at in shots:
+            hit = place == shot_at[0] - x * (rows_y * depth)
+            base = base + jnp.where(hit, shot_at[1 + step], 0.0)
+        return base
+
+    def first_plane(x, carry):
         rows = pl.ds(pl.multiple_of(x * rows_y, rows_y), rows_y)
         courant[rows, :] = jnp.broadcast_to(
             choose(classes[rows, :], entries, len(entries) // 2), (rows_y, depth)
         )
-        place = lax.broadcasted_iota(jnp.int32, (rows_y, depth), 0) * depth
-        place = place + lax.broadcasted_iota(jnp.int32, (rows_y, depth), 1)
-        here = now[rows, :]
-        base_a = 2.0 * here - old[rows, :]
-        base_b = -here
-        for spot, amp_a, amp_b in shots:
-            hit = place == spot - x * (rows_y * depth)
-            base_a = base_a + jnp.where(hit, amp_a, 0.0)
-            base_b = base_b + jnp.where(hit, amp_b, 0.0)
-        old[rows, :] = base_a
-        later[rows, :] = base_b
+        old[rows, :] = with_sources(2.0 * now[rows, :] - old[rows, :], x, 0)
         return carry
 
-    lax.fori_loop(0, rows_x, plane, 0)
+    def second_plane(x, carry):
+        rows = pl.ds(pl.multiple_of(x * rows_y, rows_y), rows_y)
+        later[rows, :] = with_sources(2.0 * mid[rows, :] - now[rows, :], x, 1)
+        return carry
+
+    lax.fori_loop(0, rows_x, first_plane, 0)
     pulls[3].wait()
     pulls[4].wait()
 
@@ -358,7 +367,7 @@
     mid_out = pltpu.make_async_copy(mid, mid_hbm, out_sem.at[0])
     mid_out.start()
 
-    later[...] = later[...] + 2.0 * mid[...]
+    lax.fori_loop(0, rows_x, second_plane, 0)
     inner(mid)
     pulls[5].wait()
     pulls[6].wait()

time: 20.4 us -> 20.3 us (level)
  no operation moved by 1% of the time
where the time goes in v6:
time: 20.3 us; the launch traced here: 20.2 us
  Pallas kernels  19.5 us (96%)
  between operations  0.64 us (3%)
    pallas_call x1, Pallas kernels, shards(): pl.pallas_call(functools.partial(kernel, rows_x, rows_y), out_shape=(out,...  18.4 us
    pallas_call x1, Pallas kernels, shards(): pl.pallas_call(put_out, out_shape=(out, out, out), in_specs=[any_spec] *...  1.17 us

profile of v6, /device:TPU:1, one launch (start us, length us, event | category | flops | bytes accessed | tf_op | source)
XLA Modules:
  0.0 20.2 jit_solution(860792480430855605)
XLA Ops:
  0.6 18.4 %shard_map.130 = (f32[256,512]{1,0:T(8,128)S(1)}, f32[256,512]{1,0:T(8,128)S(1)}, f32[256,512]{1,0:T(8,128)S(1)}) custom-call(s32[4]{0:T(128)} %cells_hbm.1, s32[4]{0:T(128)} %samples_hbm.1, f32[256]{0:T(256)} %wave_hbm.1, f32[16]{0:T(128)} %table_hbm.1, f32[256,512]{1,0:T(8,128)} %bitcast.6, f32[256,512]{1,0:T(8,128)} %bitcast.7, s32[256,512]{1,0:T(8,128)} %bitcast.8, ...), custom_call_target="tpu_custom_call" | custom-call | tf_op jit(solution)/shard_map/pallas_call | solution.py:435
  19.0 1.2 %shard_map.131 = (f32[256,512]{1,0:T(8,128)}, f32[256,512]{1,0:T(8,128)}, f32[256,512]{1,0:T(8,128)}) custom-call(f32[256,512]{1,0:T(8,128)S(1)} %get-tuple-element.9.refs_0_, f32[256,512]{1,0:T(8,128)S(1)} %get-tuple-element.10.refs_1_, f32[256,512]{1,0:T(8,128)S(1)} %get-tuple-element.11.refs_2_), custom_call_target="tpu_custom_call" | custom-call | tf_op jit(solution)/shard_map/pallas_call | solution.py:478

commit v7 on v6

--- a/solution.py
+++ b/solution.py
@@ -19,7 +19,7 @@
 QUANT_STEP = 0.5
 W = 4
 MESH = pl.DeviceIdType.MESH
-PARTS = 2
+PARTS = 4
 VMEM_BYTES = 32 * 1024 * 1024
 
 

time: 20.3 us -> 20.8 us (1.025)
  Pallas kernels: 19.5 us -> 20 us
    pallas_call x1, Pallas kernels: 18.4 us -> 18.8 us  [shards(): pl.pallas_call(functools.partial(kernel, rows_x, rows_y), out_shape=(out,...]
where the time goes in v7:
time: 20.8 us; the launch traced here: 20.6 us
  Pallas kernels  20 us (96%)
  between operations  0.64 us (3%)
    pallas_call x1, Pallas kernels, shards(): pl.pallas_call(functools.partial(kernel, rows_x, rows_y), out_shape=(out,...  18.8 us
    pallas_call x1, Pallas kernels, shards(): pl.pallas_call(put_out, out_shape=(out, out, out), in_specs=[any_spec] *...  1.17 us

profile of v7, /device:TPU:1, one launch (start us, length us, event | category | flops | bytes accessed | tf_op | source)
XLA Modules:
  0.0 20.6 jit_solution(5359839205451127128)
XLA Ops:
  0.6 18.8 %shard_map.130 = (f32[256,512]{1,0:T(8,128)S(1)}, f32[256,512]{1,0:T(8,128)S(1)}, f32[256,512]{1,0:T(8,128)S(1)}) custom-call(s32[4]{0:T(128)} %cells_hbm.1, s32[4]{0:T(128)} %samples_hbm.1, f32[256]{0:T(256)} %wave_hbm.1, f32[16]{0:T(128)} %table_hbm.1, f32[256,512]{1,0:T(8,128)} %bitcast.6, f32[256,512]{1,0:T(8,128)} %bitcast.7, s32[256,512]{1,0:T(8,128)} %bitcast.8, ...), custom_call_target="tpu_custom_call" | custom-call | tf_op jit(solution)/shard_map/pallas_call | solution.py:435
  19.5 1.2 %shard_map.131 = (f32[256,512]{1,0:T(8,128)}, f32[256,512]{1,0:T(8,128)}, f32[256,512]{1,0:T(8,128)}) custom-call(f32[256,512]{1,0:T(8,128)S(1)} %get-tuple-element.9.refs_0_, f32[256,512]{1,0:T(8,128)S(1)} %get-tuple-element.10.refs_1_, f32[256,512]{1,0:T(8,128)S(1)} %get-tuple-element.11.refs_2_), custom_call_target="tpu_custom_call" | custom-call | tf_op jit(solution)/shard_map/pallas_call | solution.py:478

commit v8 on v6

--- a/solution.py
+++ b/solution.py
@@ -149,11 +149,11 @@
     rows_x, rows_y,
     cells_hbm, samples_hbm, wave_hbm, table_hbm,
     now_hbm, old_hbm, classes_hbm, star_hbm, along_hbm, lift_hbm, sums_hbm,
-    next_hbm, mid_hbm, code_hbm,
+    later, mid, code,
     cells_ref, samples_ref, wave_ref, table_ref,
     now, old, classes, star, along, lift, sums,
-    courant, mid, later, acc, packed, bundle, halo_a, halo_b, halo_c,
-    local_sem, out_sem, send_sem, recv_sem,
+    courant, acc, packed, bundle, halo_a, halo_b, halo_c,
+    local_sem, send_sem, recv_sem,
 ):
     depth = now.shape[1]
     size = rows_x * rows_y
@@ -364,8 +364,6 @@
         mid[:, lanes] = old[:, lanes] + courant[:, lanes] * (acc[:, lanes] + outer(halo_a, lanes))
         pack(mid, 1, part)
         each(second[part][0], start)
-    mid_out = pltpu.make_async_copy(mid, mid_hbm, out_sem.at[0])
-    mid_out.start()
 
     lax.fori_loop(0, rows_x, second_plane, 0)
     inner(mid)
@@ -381,8 +379,6 @@
         bundle[:, lanes] = product((sums[0], sums[1]), both)
         each(third[part][0], start)
         lifted_own.append(both)
-    next_out = pltpu.make_async_copy(later, next_hbm, out_sem.at[1])
-    next_out.start()
 
     for lanes, both in zip(cuts, lifted_own):
         acc[:, lanes] = product([lift[0, :, :size], lift[1, :, :size]], both)
@@ -401,14 +397,9 @@
             courant[:, left] += product([half[:, :128] for half in piece], back)
     lifted = courant[...]
     shrunk = jnp.maximum(jnp.abs(lifted) - DEAD_ZONE, 0.0) / QUANT_STEP
-    acc[...] = jnp.where(lifted < 0.0, -shrunk, shrunk)
-    code_out = pltpu.make_async_copy(acc, code_hbm, out_sem.at[2])
-    code_out.start()
+    code[...] = jnp.where(lifted < 0.0, -shrunk, shrunk)
     for sends, _ in first + second + third:
         each(sends, sent)
-    mid_out.wait()
-    next_out.wait()
-    code_out.wait()
 
 
 def put_out(*refs):
@@ -436,7 +427,7 @@
         functools.partial(kernel, rows_x, rows_y),
         out_shape=(out, out, out),
         in_specs=[hbm] * 11,
-        out_specs=(any_spec,) * 3,
+        out_specs=(pl.BlockSpec(memory_space=pltpu.VMEM),) * 3,
         scratch_shapes=[
             pltpu.SMEM(source_cells.shape, jnp.int32),
             pltpu.SMEM(samples.shape, jnp.int32),
@@ -451,15 +442,12 @@
             pltpu.VMEM(sums.shape, jnp.bfloat16),
             pltpu.VMEM(flat, f32),
             pltpu.VMEM(flat, f32),
-            pltpu.VMEM(flat, f32),
-            pltpu.VMEM(flat, f32),
             pltpu.VMEM((2, 2, face_y, depth), f32),
             pltpu.VMEM((sums.shape[1], depth), f32),
             pltpu.VMEM((halo_rows, depth), f32),
             pltpu.VMEM((halo_rows, depth), f32),
             pltpu.VMEM((wide_rows, depth), f32),
             pltpu.SemaphoreType.DMA((11,)),
-            pltpu.SemaphoreType.DMA((3,)),
             pltpu.SemaphoreType.DMA((PARTS, 16)),
             pltpu.SemaphoreType.DMA((PARTS, 16)),
         ],

time: 20.3 us -> 20.3 us (level)
  no operation moved by 1% of the time
where the time goes in v8:
time: 20.3 us; the launch traced here: 20.1 us
  Pallas kernels  19.5 us (96%)
  between operations  0.64 us (3%)
    pallas_call x1, Pallas kernels, shards(): pl.pallas_call(functools.partial(kernel, rows_x, rows_y), out_shape=(out,...  18.3 us
    pallas_call x1, Pallas kernels, shards(): pl.pallas_call(put_out, out_shape=(out, out, out), in_specs=[any_spec] *...  1.17 us

profile of v8, /device:TPU:1, one launch (start us, length us, event | category | flops | bytes accessed | tf_op | source)
XLA Modules:
  0.0 20.1 jit_solution(250780757173624388)
XLA Ops:
  0.6 18.3 %shard_map.130 = (f32[256,512]{1,0:T(8,128)S(1)}, f32[256,512]{1,0:T(8,128)S(1)}, f32[256,512]{1,0:T(8,128)S(1)}) custom-call(s32[4]{0:T(128)} %cells_hbm.1, s32[4]{0:T(128)} %samples_hbm.1, f32[256]{0:T(256)} %wave_hbm.1, f32[16]{0:T(128)} %table_hbm.1, f32[256,512]{1,0:T(8,128)} %bitcast.6, f32[256,512]{1,0:T(8,128)} %bitcast.7, s32[256,512]{1,0:T(8,128)} %bitcast.8, ...), custom_call_target="tpu_custom_call" | custom-call | tf_op jit(solution)/shard_map/pallas_call | solution.py:426
  19.0 1.2 %shard_map.131 = (f32[256,512]{1,0:T(8,128)}, f32[256,512]{1,0:T(8,128)}, f32[256,512]{1,0:T(8,128)}) custom-call(f32[256,512]{1,0:T(8,128)S(1)} %get-tuple-element.9.refs_0_, f32[256,512]{1,0:T(8,128)S(1)} %get-tuple-element.10.refs_1_, f32[256,512]{1,0:T(8,128)S(1)} %get-tuple-element.11.refs_2_), custom_call_target="tpu_custom_call" | custom-call | tf_op jit(solution)/shard_map/pallas_call | solution.py:466

commit v9 on v8

--- a/solution.py
+++ b/solution.py
@@ -333,43 +333,41 @@
     pulls[3].wait()
     pulls[4].wait()
 
-    def deep(both, at, lanes):
-        return product([b[:, lanes] for b in both], [along[at, lanes, lanes], along[at + 1, lanes, lanes]])
-
-    def crossing(both, at, source, target):
-        return product(
-            [b[:, source] for b in both], [along[at, source, target], along[at + 1, source, target]]
-        )
-
     seams = [
         (slice(part * width - 128, part * width), slice(part * width, part * width + 128))
         for part in range(1, PARTS)
     ]
 
-    def inner(field):
-        both = split(field[...])
-        for lanes in cuts:
-            own = product([star[0, :, :size], star[1, :, :size]], [b[:, lanes] for b in both])
-            acc[:, lanes] = own + deep(both, 0, lanes)
-        for left, right in seams:
-            acc[:, left] += crossing(both, 0, right, left)
-            acc[:, right] += crossing(both, 0, left, right)
+    def inner(field, lanes):
+        both = split(field[:, lanes])
+        own = product([star[0, :, :size], star[1, :, :size]], both)
+        acc[:, lanes] = own + product(both, (along[0, lanes, lanes], along[1, lanes, lanes]))
+        return both
+
+    def join(halves_of):
+        for part, (left, right) in enumerate(seams):
+            below, above = halves_of[part], halves_of[part + 1]
+            over = (along[0, left, right], along[1, left, right])
+            back = (along[0, right, left], along[1, right, left])
+            acc[:, right] += product([half[:, -128:] for half in below], over)
+            acc[:, left] += product([half[:, :128] for half in above], back)
 
     def outer(halo, lanes):
         return product([star[0, :, size:], star[1, :, size:]], split(halo[:, lanes]))
 
-    inner(now)
+    join([inner(now, lanes) for lanes in cuts])
+    own_halves = []
     for part, lanes in enumerate(cuts):
         each(first[part][1], landed)
         mid[:, lanes] = old[:, lanes] + courant[:, lanes] * (acc[:, lanes] + outer(halo_a, lanes))
         pack(mid, 1, part)
         each(second[part][0], start)
+        own_halves.append(inner(mid, lanes))
 
     lax.fori_loop(0, rows_x, second_plane, 0)
-    inner(mid)
+    join(own_halves)
     pulls[5].wait()
     pulls[6].wait()
-    lifted_own = []
     for part, lanes in enumerate(cuts):
         each(second[part][1], landed)
         later[:, lanes] = later[:, lanes] + courant[:, lanes] * (
@@ -378,10 +376,8 @@
         both = split(later[:, lanes])
         bundle[:, lanes] = product((sums[0], sums[1]), both)
         each(third[part][0], start)
-        lifted_own.append(both)
-
-    for lanes, both in zip(cuts, lifted_own):
         acc[:, lanes] = product([lift[0, :, :size], lift[1, :, :size]], both)
+
     pieces = []
     for part, lanes in enumerate(cuts):
         each(third[part][1], landed)

time: 20.3 us -> 20.3 us (level)
  no operation moved by 1% of the time
where the time goes in v9:
time: 20.3 us; the launch traced here: 20.1 us
  Pallas kernels  19.5 us (96%)
  between operations  0.64 us (3%)
    pallas_call x1, Pallas kernels, shards(): pl.pallas_call(functools.partial(kernel, rows_x, rows_y), out_shape=(out,...  18.3 us
    pallas_call x1, Pallas kernels, shards(): pl.pallas_call(put_out, out_shape=(out, out, out), in_specs=[any_spec] *...  1.17 us

profile of v9, /device:TPU:1, one launch (start us, length us, event | category | flops | bytes accessed | tf_op | source)
XLA Modules:
  0.0 20.1 jit_solution(4342376825338660261)
XLA Ops:
  0.6 18.3 %shard_map.130 = (f32[256,512]{1,0:T(8,128)S(1)}, f32[256,512]{1,0:T(8,128)S(1)}, f32[256,512]{1,0:T(8,128)S(1)}) custom-call(s32[4]{0:T(128)} %cells_hbm.1, s32[4]{0:T(128)} %samples_hbm.1, f32[256]{0:T(256)} %wave_hbm.1, f32[16]{0:T(128)} %table_hbm.1, f32[256,512]{1,0:T(8,128)} %bitcast.6, f32[256,512]{1,0:T(8,128)} %bitcast.7, s32[256,512]{1,0:T(8,128)} %bitcast.8, ...), custom_call_target="tpu_custom_call" | custom-call | tf_op jit(solution)/shard_map/pallas_call | solution.py:422
  19.0 1.2 %shard_map.131 = (f32[256,512]{1,0:T(8,128)}, f32[256,512]{1,0:T(8,128)}, f32[256,512]{1,0:T(8,128)}) custom-call(f32[256,512]{1,0:T(8,128)S(1)} %get-tuple-element.9.refs_0_, f32[256,512]{1,0:T(8,128)S(1)} %get-tuple-element.10.refs_1_, f32[256,512]{1,0:T(8,128)S(1)} %get-tuple-element.11.refs_2_), custom_call_target="tpu_custom_call" | custom-call | tf_op jit(solution)/shard_map/pallas_call | solution.py:462
